TPU v7x, 256 devices: a whole 4x4x8 slice. The times are simulated.
256 devices in a mesh: head: 8 (over x_lo, y), blk: 32 (over z, x_hi, core).
Axes of the slice: x: 4 (x_hi: 2, x_lo: 2; x = x_hi * 2 + x_lo), y: 4, z: 8, core: 2. Of those that a mesh axis runs over, the one named last changes fastest.
Arguments:
- queries: bfloat16 [8192, 4096], P(('head', 'blk')), may hold values from -6 to 6
- key_heads: bfloat16 [8192, 512], P(('head', 'blk')), may hold values from -6 to 6
- value_heads: bfloat16 [8192, 512], P(('head', 'blk')), may hold values from -6 to 6
- outputs: bfloat16 [8192, 4096], P(('head', 'blk')), may hold values from -6 to 6
- out_grad: bfloat16 [8192, 4096], P(('head', 'blk')), may hold values from -6 to 6
- log_total: bfloat16 [8192, 32], P(('head', 'blk')), may hold values from 0 to 20
- positions: int32 [32, 256], replicated, may hold values from 0 to 8191, as said below
Outputs:
- query_grad: bfloat16 [8192, 4096], P(('head', 'blk'))
- key_grad: bfloat16 [8192, 512], P(('head', 'blk'))
- value_grad: bfloat16 [8192, 512], P(('head', 'blk'))
Inputs may be any that keep to these rules, and one draw needn't show every extreme that they name: Every position 0 to 8191 appears once. Each row of positions is two runs of 128 consecutive rising positions, each run starting at a multiple of its length.
All inputs are finite; a program needn't handle non-finite values.
Results may differ from a plain program's by a relative error of at most 0.012.
Values may be sent and summed in bfloat16 or wider, within the bound.
A program may use at most 64 MiB of HBM per device.

v0:
```python
import math

import jax
import jax.numpy as jnp
from jax import lax
from jax.sharding import PartitionSpec as P

D = 128
GROUP = 8
HQ = 32


def passed_along(value, axis, steps):
    count = lax.axis_size(axis)
    pairs = [(source, (source + steps) % count) for source in range(count)]
    return lax.ppermute(value, axis, pairs)


def shards(queries, key_heads, value_heads, outputs, out_grad, log_total, positions):
    head_count = lax.axis_size("head")
    cycle_count = lax.axis_size("blk")
    tokens_here = queries.shape[0]
    kv_count = HQ // GROUP
    share = head_count // kv_count
    heads_here = HQ // head_count
    rows = tokens_here * head_count
    half = rows // 2
    scale = 1.0 / math.sqrt(D)

    def widen(block_in):
        return jnp.repeat(block_in.reshape(tokens_here, kv_count, D), GROUP, axis=1).reshape(
            tokens_here, HQ * D
        )

    query_flat, output_flat, grad_flat, log_flat, key_wide, value_wide = (
        lax.all_to_all(queries, "head", split_axis=1, concat_axis=0, tiled=True),
        lax.all_to_all(outputs, "head", split_axis=1, concat_axis=0, tiled=True),
        lax.all_to_all(out_grad, "head", split_axis=1, concat_axis=0, tiled=True),
        lax.all_to_all(log_total, "head", split_axis=1, concat_axis=0, tiled=True),
        lax.all_to_all(widen(key_heads), "head", split_axis=1, concat_axis=0, tiled=True),
        lax.all_to_all(widen(value_heads), "head", split_axis=1, concat_axis=0, tiled=True),
    )
    key_rows = key_wide[:, :D]
    value_rows = value_wide[:, :D]
    query_rows = query_flat.reshape(rows, heads_here, D)
    grad_rows = grad_flat.reshape(rows, heads_here, D)
    log_rows = log_flat.astype(jnp.float32)
    delta_rows = jnp.sum(
        output_flat.reshape(rows, heads_here, D).astype(jnp.float32)
        * grad_rows.astype(jnp.float32),
        axis=2,
    )
    flat_pos = positions.reshape(-1)
    cycle_index = lax.axis_index("blk")
    query_pos = lax.dynamic_slice_in_dim(flat_pos, cycle_index * rows, rows)

    def pair_terms(query_run, key_part, value_part, pos_part):
        query_block = query_rows[query_run * half : (query_run + 1) * half]
        grad_block = grad_rows[query_run * half : (query_run + 1) * half]
        log_block = log_rows[query_run * half : (query_run + 1) * half]
        delta_block = delta_rows[query_run * half : (query_run + 1) * half]
        pos_block = query_pos[query_run * half : (query_run + 1) * half]

        def live():
            scores = (
                jnp.einsum("qhd,kd->qhk", query_block, key_part, preferred_element_type=jnp.float32)
                * scale
            )
            mask = pos_block[:, None, None] >= pos_part[None, None, :]
            probs = jnp.where(mask, jnp.exp(scores - log_block[..., None]), 0.0)
            value_term = jnp.einsum(
                "qhk,qhd->kd",
                probs.astype(jnp.bfloat16),
                grad_block,
                preferred_element_type=jnp.float32,
            )
            prob_grad = jnp.einsum(
                "qhd,kd->qhk", grad_block, value_part, preferred_element_type=jnp.float32
            )
            score_grad = (probs * (prob_grad - delta_block[..., None])).astype(jnp.bfloat16)
            query_term = (
                jnp.einsum("qhk,kd->qhd", score_grad, key_part, preferred_element_type=jnp.float32)
                * scale
            )
            key_term = (
                jnp.einsum(
                    "qhk,qhd->kd", score_grad, query_block, preferred_element_type=jnp.float32
                )
                * scale
            )
            return (query_term, key_term, value_term)

        def quiet():
            return (
                jnp.zeros((half, heads_here, D), jnp.float32),
                jnp.zeros((half, D), jnp.float32),
                jnp.zeros((half, D), jnp.float32),
            )

        return lax.cond(jnp.max(pos_block) >= jnp.min(pos_part), live, quiet)

    def shard_terms(key_block, value_block, key_pos):
        query_terms = [jnp.zeros((half, heads_here, D), jnp.float32) for query_run in range(2)]
        key_terms = []
        value_terms = []
        for column in range(2):
            key_part = key_block[column * half : (column + 1) * half]
            value_part = value_block[column * half : (column + 1) * half]
            pos_part = key_pos[column * half : (column + 1) * half]
            key_sum = jnp.zeros((half, D), jnp.float32)
            value_sum = jnp.zeros((half, D), jnp.float32)
            for query_run in range(2):
                query_term, key_term, value_term = pair_terms(
                    query_run, key_part, value_part, pos_part
                )
                query_terms[query_run] = query_terms[query_run] + query_term
                key_sum = key_sum + key_term
                value_sum = value_sum + value_term
            key_terms.append(key_sum)
            value_terms.append(value_sum)
        return (
            jnp.concatenate(query_terms, axis=0),
            jnp.concatenate(key_terms, axis=0),
            jnp.concatenate(value_terms, axis=0),
        )

    empty_kv = jnp.zeros((rows, D), jnp.float32)
    empty_query = jnp.zeros((rows, heads_here, D), jnp.float32)

    def cycle_step(step, carry):
        key_block, value_block, key_acc, value_acc, query_acc = carry
        source = (cycle_index - step) % cycle_count
        key_pos = lax.dynamic_slice_in_dim(flat_pos, source * rows, rows)
        query_term, key_term, value_term = shard_terms(key_block, value_block, key_pos)
        key_block, value_block = passed_along((key_block, value_block), "blk", 1)
        key_acc, value_acc = passed_along((key_acc + key_term, value_acc + value_term), "blk", 1)
        return (key_block, value_block, key_acc, value_acc, query_acc + query_term)

    final = lax.fori_loop(
        0, cycle_count, cycle_step, (key_rows, value_rows, empty_kv, empty_kv, empty_query)
    )
    key_acc, value_acc, query_acc = (final[2], final[3], final[4])
    query_seq, key_seq, value_seq = (
        lax.all_to_all(
            query_acc.reshape(rows, heads_here * D).astype(jnp.bfloat16),
            "head",
            split_axis=0,
            concat_axis=1,
            tiled=True,
        ).astype(jnp.float32),
        lax.all_to_all(
            key_acc.astype(jnp.bfloat16), "head", split_axis=0, concat_axis=1, tiled=True
        ).astype(key_acc.dtype),
        lax.all_to_all(
            value_acc.astype(jnp.bfloat16), "head", split_axis=0, concat_axis=1, tiled=True
        ).astype(value_acc.dtype),
    )
    key_out = (
        key_seq.reshape(tokens_here, kv_count, share, D)
        .sum(axis=2)
        .reshape(tokens_here, kv_count * D)
    )
    value_out = (
        value_seq.reshape(tokens_here, kv_count, share, D)
        .sum(axis=2)
        .reshape(tokens_here, kv_count * D)
    )
    return (
        query_seq.astype(jnp.bfloat16),
        key_out.astype(jnp.bfloat16),
        value_out.astype(jnp.bfloat16),
    )


def solution(mesh):
    in_specs = (
        P(("head", "blk"), None),
        P(("head", "blk"), None),
        P(("head", "blk"), None),
        P(("head", "blk"), None),
        P(("head", "blk"), None),
        P(("head", "blk"), None),
        P(),
    )
    out_specs = (P(("head", "blk"), None), P(("head", "blk"), None), P(("head", "blk"), None))
    return jax.shard_map(shards, mesh=mesh, in_specs=in_specs, out_specs=out_specs, check_vma=False)
```

profile of v0, /device:TPU:1, one launch (start us, length us, event | category | flops | bytes accessed | tf_op | source)
XLA Modules:
  0.0 705.8 jit_solution(9230007955546620333)
XLA Ops:
  2.0 5.9 all-to-all-start.3
  9.0 4.0 all-to-all-done.3
  17.5 5.0 all-to-all-done.1
  26.6 5.3 all-to-all-done
  36.3 5.2 all-to-all-done.2
  46.6 4.4 all-to-all-done.5
  54.6 5.8 all-to-all-done.4
  61.0 617.1 %while.24 = (s32[]{:T(128)}, bf16[256,128]{1,0:T(8,128)(2,1)S(1)}, bf16[256,128]{1,0:T(8,128)(2,1)S(1)}, f32[256,128]{1,0:T(8,128)S(1)}, f32[256,128]{1,0:T(8,12...) while((s32[]{:T(128)}, bf16[256,128]{1,0:T(8,128)(2,1)S(1)}, ...), condition=%wide.region_14.15_spmd.clone, body=%wide.region_3.14_spmd.clone.sunk | while | flops 338493696 | bytes 16821168 | solution.py:139
  61.0 10.3 %collective-permute-start = (bf16[256,128]{1,0:T(8,128)(2,1)S(1)}, bf16[256,128]{1,0:T(8,128)(2,1)S(1)}, u32[]{:S(2)}, u32[]{:S(2)}) collective-permute-start(bf16[256,128]{1,0:T(8,128)(2,1)S(1)} %copy.149), channel_id=1, source_target_pairs={{0,1},{1,2},{2,3},{3,4},{4,5},{5,6},{6,7},{7,8},{8,9},{9,10},{10,1... | collective-permute-start | bytes 196616 | tf_op jit(solution)/shard_map/while/body/eval_jaxpr/ppermute | solution.py:16
  107.0 4.0 collective-permute-start
  118.3 4.4 collective-permute-start.3
  155.7 6.7 collective-permute-start.3
  165.7 4.0 collective-permute-start
  183.6 4.0 collective-permute-start
  194.9 5.0 collective-permute-start.3
  242.8 4.0 collective-permute-start
  253.0 5.3 collective-permute-start.3
  289.5 5.7 collective-permute-start.3
  336.0 4.0 collective-permute-start
  369.7 4.0 collective-permute-start
  422.6 4.3 collective-permute-start.3
  448.1 4.0 collective-permute-start
  458.3 6.6 collective-permute-start.3
  468.2 4.0 collective-permute-start
  504.4 4.0 collective-permute-start
  517.8 7.1 %collective-permute-start.3 = (f32[256,128]{1,0:T(8,128)S(1)}, f32[256,128]{1,0:T(8,128)S(1)}, u32[]{:S(2)}, u32[]{:S(2)}) collective-permute-start(f32[256,128]{1,0:T(8,128)S(1)} %maximum_add_fusion.7), channel_id=1, source_target_pairs={{0,1},{1,2},{2,3},{3,4},{4,5},{5,6},{6,7},{7,8},{8,9},{9,10},{10,1... | collective-permute-start | bytes 393224 | tf_op jit(solution)/shard_map/while/body/eval_jaxpr/ppermute | solution.py:16
  574.8 5.0 collective-permute-start.3
  612.6 5.4 collective-permute-start.3
  631.7 7.2 %collective-permute-start.3 = (f32[256,128]{1,0:T(8,128)S(1)}, f32[256,128]{1,0:T(8,128)S(1)}, u32[]{:S(2)}, u32[]{:S(2)}) collective-permute-start(f32[256,128]{1,0:T(8,128)S(1)} %maximum_add_fusion.7), channel_id=1, source_target_pairs={{0,1},{1,2},{2,3},{3,4},{4,5},{5,6},{6,7},{7,8},{8,9},{9,10},{10,1... | collective-permute-start | bytes 393224 | tf_op jit(solution)/shard_map/while/body/eval_jaxpr/ppermute | solution.py:16
  642.2 4.0 collective-permute-start
  691.2 4.5 all-to-all-done.8
  699.7 5.4 all-to-all-done.6
  (1520 shorter events, 448.8 us)
Async XLA Ops:
  61.0 22.5 %collective-permute-start = (bf16[256,128]{1,0:T(8,128)(2,1)S(1)}, bf16[256,128]{1,0:T(8,128)(2,1)S(1)}, u32[]{:S(2)}, u32[]{:S(2)}) collective-permute-start(bf16[256,128]{1,0:T(8,128)(2,1)S(1)} %copy.149), channel_id=1, source_target_pairs={{0,1},{1,2},{2,3},{3,4},{4,5},{5,6},{6,7},{7,8},{8,9},{9,10},{10,1... | collective-permute-start | bytes 196616 | tf_op jit(solution)/shard_map/while/body/eval_jaxpr/ppermute | solution.py:16
  86.4 17.6 %collective-permute-start = (bf16[256,128]{1,0:T(8,128)(2,1)S(1)}, bf16[256,128]{1,0:T(8,128)(2,1)S(1)}, u32[]{:S(2)}, u32[]{:S(2)}) collective-permute-start(bf16[256,128]{1,0:T(8,128)(2,1)S(1)} %copy.149), channel_id=1, source_target_pairs={{0,1},{1,2},{2,3},{3,4},{4,5},{5,6},{6,7},{7,8},{8,9},{9,10},{10,1... | collective-permute-start | bytes 196616 | tf_op jit(solution)/shard_map/while/body/eval_jaxpr/ppermute | solution.py:16
  107.0 16.2 %collective-permute-start = (bf16[256,128]{1,0:T(8,128)(2,1)S(1)}, bf16[256,128]{1,0:T(8,128)(2,1)S(1)}, u32[]{:S(2)}, u32[]{:S(2)}) collective-permute-start(bf16[256,128]{1,0:T(8,128)(2,1)S(1)} %copy.149), channel_id=1, source_target_pairs={{0,1},{1,2},{2,3},{3,4},{4,5},{5,6},{6,7},{7,8},{8,9},{9,10},{10,1... | collective-permute-start | bytes 196616 | tf_op jit(solution)/shard_map/while/body/eval_jaxpr/ppermute | solution.py:16
  126.0 16.5 %collective-permute-start = (bf16[256,128]{1,0:T(8,128)(2,1)S(1)}, bf16[256,128]{1,0:T(8,128)(2,1)S(1)}, u32[]{:S(2)}, u32[]{:S(2)}) collective-permute-start(bf16[256,128]{1,0:T(8,128)(2,1)S(1)} %copy.149), channel_id=1, source_target_pairs={{0,1},{1,2},{2,3},{3,4},{4,5},{5,6},{6,7},{7,8},{8,9},{9,10},{10,1... | collective-permute-start | bytes 196616 | tf_op jit(solution)/shard_map/while/body/eval_jaxpr/ppermute | solution.py:16
  144.3 18.4 %collective-permute-start = (bf16[256,128]{1,0:T(8,128)(2,1)S(1)}, bf16[256,128]{1,0:T(8,128)(2,1)S(1)}, u32[]{:S(2)}, u32[]{:S(2)}) collective-permute-start(bf16[256,128]{1,0:T(8,128)(2,1)S(1)} %copy.149), channel_id=1, source_target_pairs={{0,1},{1,2},{2,3},{3,4},{4,5},{5,6},{6,7},{7,8},{8,9},{9,10},{10,1... | collective-permute-start | bytes 196616 | tf_op jit(solution)/shard_map/while/body/eval_jaxpr/ppermute | solution.py:16
  165.7 15.0 %collective-permute-start = (bf16[256,128]{1,0:T(8,128)(2,1)S(1)}, bf16[256,128]{1,0:T(8,128)(2,1)S(1)}, u32[]{:S(2)}, u32[]{:S(2)}) collective-permute-start(bf16[256,128]{1,0:T(8,128)(2,1)S(1)} %copy.149), channel_id=1, source_target_pairs={{0,1},{1,2},{2,3},{3,4},{4,5},{5,6},{6,7},{7,8},{8,9},{9,10},{10,1... | collective-permute-start | bytes 196616 | tf_op jit(solution)/shard_map/while/body/eval_jaxpr/ppermute | solution.py:16
  183.6 16.7 %collective-permute-start = (bf16[256,128]{1,0:T(8,128)(2,1)S(1)}, bf16[256,128]{1,0:T(8,128)(2,1)S(1)}, u32[]{:S(2)}, u32[]{:S(2)}) collective-permute-start(bf16[256,128]{1,0:T(8,128)(2,1)S(1)} %copy.149), channel_id=1, source_target_pairs={{0,1},{1,2},{2,3},{3,4},{4,5},{5,6},{6,7},{7,8},{8,9},{9,10},{10,1... | collective-permute-start | bytes 196616 | tf_op jit(solution)/shard_map/while/body/eval_jaxpr/ppermute | solution.py:16
  203.2 17.8 %collective-permute-start = (bf16[256,128]{1,0:T(8,128)(2,1)S(1)}, bf16[256,128]{1,0:T(8,128)(2,1)S(1)}, u32[]{:S(2)}, u32[]{:S(2)}) collective-permute-start(bf16[256,128]{1,0:T(8,128)(2,1)S(1)} %copy.149), channel_id=1, source_target_pairs={{0,1},{1,2},{2,3},{3,4},{4,5},{5,6},{6,7},{7,8},{8,9},{9,10},{10,1... | collective-permute-start | bytes 196616 | tf_op jit(solution)/shard_map/while/body/eval_jaxpr/ppermute | solution.py:16
  223.9 16.0 %collective-permute-start = (bf16[256,128]{1,0:T(8,128)(2,1)S(1)}, bf16[256,128]{1,0:T(8,128)(2,1)S(1)}, u32[]{:S(2)}, u32[]{:S(2)}) collective-permute-start(bf16[256,128]{1,0:T(8,128)(2,1)S(1)} %copy.149), channel_id=1, source_target_pairs={{0,1},{1,2},{2,3},{3,4},{4,5},{5,6},{6,7},{7,8},{8,9},{9,10},{10,1... | collective-permute-start | bytes 196616 | tf_op jit(solution)/shard_map/while/body/eval_jaxpr/ppermute | solution.py:16
  242.8 16.0 %collective-permute-start = (bf16[256,128]{1,0:T(8,128)(2,1)S(1)}, bf16[256,128]{1,0:T(8,128)(2,1)S(1)}, u32[]{:S(2)}, u32[]{:S(2)}) collective-permute-start(bf16[256,128]{1,0:T(8,128)(2,1)S(1)} %copy.149), channel_id=1, source_target_pairs={{0,1},{1,2},{2,3},{3,4},{4,5},{5,6},{6,7},{7,8},{8,9},{9,10},{10,1... | collective-permute-start | bytes 196616 | tf_op jit(solution)/shard_map/while/body/eval_jaxpr/ppermute | solution.py:16
  261.6 16.0 %collective-permute-start = (bf16[256,128]{1,0:T(8,128)(2,1)S(1)}, bf16[256,128]{1,0:T(8,128)(2,1)S(1)}, u32[]{:S(2)}, u32[]{:S(2)}) collective-permute-start(bf16[256,128]{1,0:T(8,128)(2,1)S(1)} %copy.149), channel_id=1, source_target_pairs={{0,1},{1,2},{2,3},{3,4},{4,5},{5,6},{6,7},{7,8},{8,9},{9,10},{10,1... | collective-permute-start | bytes 196616 | tf_op jit(solution)/shard_map/while/body/eval_jaxpr/ppermute | solution.py:16
  279.3 16.3 %collective-permute-start = (bf16[256,128]{1,0:T(8,128)(2,1)S(1)}, bf16[256,128]{1,0:T(8,128)(2,1)S(1)}, u32[]{:S(2)}, u32[]{:S(2)}) collective-permute-start(bf16[256,128]{1,0:T(8,128)(2,1)S(1)} %copy.149), channel_id=1, source_target_pairs={{0,1},{1,2},{2,3},{3,4},{4,5},{5,6},{6,7},{7,8},{8,9},{9,10},{10,1... | collective-permute-start | bytes 196616 | tf_op jit(solution)/shard_map/while/body/eval_jaxpr/ppermute | solution.py:16
  298.6 17.7 %collective-permute-start = (bf16[256,128]{1,0:T(8,128)(2,1)S(1)}, bf16[256,128]{1,0:T(8,128)(2,1)S(1)}, u32[]{:S(2)}, u32[]{:S(2)}) collective-permute-start(bf16[256,128]{1,0:T(8,128)(2,1)S(1)} %copy.149), channel_id=1, source_target_pairs={{0,1},{1,2},{2,3},{3,4},{4,5},{5,6},{6,7},{7,8},{8,9},{9,10},{10,1... | collective-permute-start | bytes 196616 | tf_op jit(solution)/shard_map/while/body/eval_jaxpr/ppermute | solution.py:16
  318.0 15.0 %collective-permute-start = (bf16[256,128]{1,0:T(8,128)(2,1)S(1)}, bf16[256,128]{1,0:T(8,128)(2,1)S(1)}, u32[]{:S(2)}, u32[]{:S(2)}) collective-permute-start(bf16[256,128]{1,0:T(8,128)(2,1)S(1)} %copy.149), channel_id=1, source_target_pairs={{0,1},{1,2},{2,3},{3,4},{4,5},{5,6},{6,7},{7,8},{8,9},{9,10},{10,1... | collective-permute-start | bytes 196616 | tf_op jit(solution)/shard_map/while/body/eval_jaxpr/ppermute | solution.py:16
  369.7 18.9 %collective-permute-start = (bf16[256,128]{1,0:T(8,128)(2,1)S(1)}, bf16[256,128]{1,0:T(8,128)(2,1)S(1)}, u32[]{:S(2)}, u32[]{:S(2)}) collective-permute-start(bf16[256,128]{1,0:T(8,128)(2,1)S(1)} %copy.149), channel_id=1, source_target_pairs={{0,1},{1,2},{2,3},{3,4},{4,5},{5,6},{6,7},{7,8},{8,9},{9,10},{10,1... | collective-permute-start | bytes 196616 | tf_op jit(solution)/shard_map/while/body/eval_jaxpr/ppermute | solution.py:16
  373.7 14.9 %collective-permute-start.1 = (bf16[256,128]{1,0:T(8,128)(2,1)S(1)}, bf16[256,128]{1,0:T(8,128)(2,1)S(1)}, u32[]{:S(2)}, u32[]{:S(2)}) collective-permute-start(bf16[256,128]{1,0:T(8,128)(2,1)S(1)} %copy.150), channel_id=1, source_target_pairs={{0,1},{1,2},{2,3},{3,4},{4,5},{5,6},{6,7},{7,8},{8,9},{9,10},{10,1... | collective-permute-start | bytes 196616 | tf_op jit(solution)/shard_map/while/body/eval_jaxpr/ppermute | solution.py:16
  391.5 15.8 %collective-permute-start = (bf16[256,128]{1,0:T(8,128)(2,1)S(1)}, bf16[256,128]{1,0:T(8,128)(2,1)S(1)}, u32[]{:S(2)}, u32[]{:S(2)}) collective-permute-start(bf16[256,128]{1,0:T(8,128)(2,1)S(1)} %copy.149), channel_id=1, source_target_pairs={{0,1},{1,2},{2,3},{3,4},{4,5},{5,6},{6,7},{7,8},{8,9},{9,10},{10,1... | collective-permute-start | bytes 196616 | tf_op jit(solution)/shard_map/while/body/eval_jaxpr/ppermute | solution.py:16
  410.2 17.2 %collective-permute-start = (bf16[256,128]{1,0:T(8,128)(2,1)S(1)}, bf16[256,128]{1,0:T(8,128)(2,1)S(1)}, u32[]{:S(2)}, u32[]{:S(2)}) collective-permute-start(bf16[256,128]{1,0:T(8,128)(2,1)S(1)} %copy.149), channel_id=1, source_target_pairs={{0,1},{1,2},{2,3},{3,4},{4,5},{5,6},{6,7},{7,8},{8,9},{9,10},{10,1... | collective-permute-start | bytes 196616 | tf_op jit(solution)/shard_map/while/body/eval_jaxpr/ppermute | solution.py:16
  430.3 15.0 %collective-permute-start = (bf16[256,128]{1,0:T(8,128)(2,1)S(1)}, bf16[256,128]{1,0:T(8,128)(2,1)S(1)}, u32[]{:S(2)}, u32[]{:S(2)}) collective-permute-start(bf16[256,128]{1,0:T(8,128)(2,1)S(1)} %copy.149), channel_id=1, source_target_pairs={{0,1},{1,2},{2,3},{3,4},{4,5},{5,6},{6,7},{7,8},{8,9},{9,10},{10,1... | collective-permute-start | bytes 196616 | tf_op jit(solution)/shard_map/while/body/eval_jaxpr/ppermute | solution.py:16
  448.1 17.2 %collective-permute-start = (bf16[256,128]{1,0:T(8,128)(2,1)S(1)}, bf16[256,128]{1,0:T(8,128)(2,1)S(1)}, u32[]{:S(2)}, u32[]{:S(2)}) collective-permute-start(bf16[256,128]{1,0:T(8,128)(2,1)S(1)} %copy.149), channel_id=1, source_target_pairs={{0,1},{1,2},{2,3},{3,4},{4,5},{5,6},{6,7},{7,8},{8,9},{9,10},{10,1... | collective-permute-start | bytes 196616 | tf_op jit(solution)/shard_map/while/body/eval_jaxpr/ppermute | solution.py:16
  468.2 15.0 %collective-permute-start = (bf16[256,128]{1,0:T(8,128)(2,1)S(1)}, bf16[256,128]{1,0:T(8,128)(2,1)S(1)}, u32[]{:S(2)}, u32[]{:S(2)}) collective-permute-start(bf16[256,128]{1,0:T(8,128)(2,1)S(1)} %copy.149), channel_id=1, source_target_pairs={{0,1},{1,2},{2,3},{3,4},{4,5},{5,6},{6,7},{7,8},{8,9},{9,10},{10,1... | collective-permute-start | bytes 196616 | tf_op jit(solution)/shard_map/while/body/eval_jaxpr/ppermute | solution.py:16
  485.0 16.4 %collective-permute-start = (bf16[256,128]{1,0:T(8,128)(2,1)S(1)}, bf16[256,128]{1,0:T(8,128)(2,1)S(1)}, u32[]{:S(2)}, u32[]{:S(2)}) collective-permute-start(bf16[256,128]{1,0:T(8,128)(2,1)S(1)} %copy.149), channel_id=1, source_target_pairs={{0,1},{1,2},{2,3},{3,4},{4,5},{5,6},{6,7},{7,8},{8,9},{9,10},{10,1... | collective-permute-start | bytes 196616 | tf_op jit(solution)/shard_map/while/body/eval_jaxpr/ppermute | solution.py:16
  504.4 21.0 %collective-permute-start = (bf16[256,128]{1,0:T(8,128)(2,1)S(1)}, bf16[256,128]{1,0:T(8,128)(2,1)S(1)}, u32[]{:S(2)}, u32[]{:S(2)}) collective-permute-start(bf16[256,128]{1,0:T(8,128)(2,1)S(1)} %copy.149), channel_id=1, source_target_pairs={{0,1},{1,2},{2,3},{3,4},{4,5},{5,6},{6,7},{7,8},{8,9},{9,10},{10,1... | collective-permute-start | bytes 196616 | tf_op jit(solution)/shard_map/while/body/eval_jaxpr/ppermute | solution.py:16
  508.3 17.1 %collective-permute-start.1 = (bf16[256,128]{1,0:T(8,128)(2,1)S(1)}, bf16[256,128]{1,0:T(8,128)(2,1)S(1)}, u32[]{:S(2)}, u32[]{:S(2)}) collective-permute-start(bf16[256,128]{1,0:T(8,128)(2,1)S(1)} %copy.150), channel_id=1, source_target_pairs={{0,1},{1,2},{2,3},{3,4},{4,5},{5,6},{6,7},{7,8},{8,9},{9,10},{10,1... | collective-permute-start | bytes 196616 | tf_op jit(solution)/shard_map/while/body/eval_jaxpr/ppermute | solution.py:16
  545.3 14.9 %collective-permute-start = (bf16[256,128]{1,0:T(8,128)(2,1)S(1)}, bf16[256,128]{1,0:T(8,128)(2,1)S(1)}, u32[]{:S(2)}, u32[]{:S(2)}) collective-permute-start(bf16[256,128]{1,0:T(8,128)(2,1)S(1)} %copy.149), channel_id=1, source_target_pairs={{0,1},{1,2},{2,3},{3,4},{4,5},{5,6},{6,7},{7,8},{8,9},{9,10},{10,1... | collective-permute-start | bytes 196616 | tf_op jit(solution)/shard_map/while/body/eval_jaxpr/ppermute | solution.py:16
  561.9 18.2 %collective-permute-start = (bf16[256,128]{1,0:T(8,128)(2,1)S(1)}, bf16[256,128]{1,0:T(8,128)(2,1)S(1)}, u32[]{:S(2)}, u32[]{:S(2)}) collective-permute-start(bf16[256,128]{1,0:T(8,128)(2,1)S(1)} %copy.149), channel_id=1, source_target_pairs={{0,1},{1,2},{2,3},{3,4},{4,5},{5,6},{6,7},{7,8},{8,9},{9,10},{10,1... | collective-permute-start | bytes 196616 | tf_op jit(solution)/shard_map/while/body/eval_jaxpr/ppermute | solution.py:16
  583.1 16.4 %collective-permute-start = (bf16[256,128]{1,0:T(8,128)(2,1)S(1)}, bf16[256,128]{1,0:T(8,128)(2,1)S(1)}, u32[]{:S(2)}, u32[]{:S(2)}) collective-permute-start(bf16[256,128]{1,0:T(8,128)(2,1)S(1)} %copy.149), channel_id=1, source_target_pairs={{0,1},{1,2},{2,3},{3,4},{4,5},{5,6},{6,7},{7,8},{8,9},{9,10},{10,1... | collective-permute-start | bytes 196616 | tf_op jit(solution)/shard_map/while/body/eval_jaxpr/ppermute | solution.py:16
  602.4 16.2 %collective-permute-start = (bf16[256,128]{1,0:T(8,128)(2,1)S(1)}, bf16[256,128]{1,0:T(8,128)(2,1)S(1)}, u32[]{:S(2)}, u32[]{:S(2)}) collective-permute-start(bf16[256,128]{1,0:T(8,128)(2,1)S(1)} %copy.149), channel_id=1, source_target_pairs={{0,1},{1,2},{2,3},{3,4},{4,5},{5,6},{6,7},{7,8},{8,9},{9,10},{10,1... | collective-permute-start | bytes 196616 | tf_op jit(solution)/shard_map/while/body/eval_jaxpr/ppermute | solution.py:16
  621.4 19.0 %collective-permute-start = (bf16[256,128]{1,0:T(8,128)(2,1)S(1)}, bf16[256,128]{1,0:T(8,128)(2,1)S(1)}, u32[]{:S(2)}, u32[]{:S(2)}) collective-permute-start(bf16[256,128]{1,0:T(8,128)(2,1)S(1)} %copy.149), channel_id=1, source_target_pairs={{0,1},{1,2},{2,3},{3,4},{4,5},{5,6},{6,7},{7,8},{8,9},{9,10},{10,1... | collective-permute-start | bytes 196616 | tf_op jit(solution)/shard_map/while/body/eval_jaxpr/ppermute | solution.py:16
  625.4 15.0 %collective-permute-start.1 = (bf16[256,128]{1,0:T(8,128)(2,1)S(1)}, bf16[256,128]{1,0:T(8,128)(2,1)S(1)}, u32[]{:S(2)}, u32[]{:S(2)}) collective-permute-start(bf16[256,128]{1,0:T(8,128)(2,1)S(1)} %copy.150), channel_id=1, source_target_pairs={{0,1},{1,2},{2,3},{3,4},{4,5},{5,6},{6,7},{7,8},{8,9},{9,10},{10,1... | collective-permute-start | bytes 196616 | tf_op jit(solution)/shard_map/while/body/eval_jaxpr/ppermute | solution.py:16
  642.2 14.9 %collective-permute-start = (bf16[256,128]{1,0:T(8,128)(2,1)S(1)}, bf16[256,128]{1,0:T(8,128)(2,1)S(1)}, u32[]{:S(2)}, u32[]{:S(2)}) collective-permute-start(bf16[256,128]{1,0:T(8,128)(2,1)S(1)} %copy.149), channel_id=1, source_target_pairs={{0,1},{1,2},{2,3},{3,4},{4,5},{5,6},{6,7},{7,8},{8,9},{9,10},{10,1... | collective-permute-start | bytes 196616 | tf_op jit(solution)/shard_map/while/body/eval_jaxpr/ppermute | solution.py:16
  660.0 15.1 %collective-permute-start = (bf16[256,128]{1,0:T(8,128)(2,1)S(1)}, bf16[256,128]{1,0:T(8,128)(2,1)S(1)}, u32[]{:S(2)}, u32[]{:S(2)}) collective-permute-start(bf16[256,128]{1,0:T(8,128)(2,1)S(1)} %copy.149), channel_id=1, source_target_pairs={{0,1},{1,2},{2,3},{3,4},{4,5},{5,6},{6,7},{7,8},{8,9},{9,10},{10,1... | collective-permute-start | bytes 196616 | tf_op jit(solution)/shard_map/while/body/eval_jaxpr/ppermute | solution.py:16
  (111 other events, 794.5 us)
where the time goes:
time: 716 us; the launch traced here: 706 us
  starting transfers between devices  297 us (41%)
  loops' own time  168 us (23%)
  waiting for transfers between devices  128 us (18%)
  matrix products  57.4 us (8%)
  other arithmetic  38.2 us (5%)
  local copies, waits for them, and re-layouts  16.1 us (2%)
    ppermute x128, starting transfers between devices, passed_along(): return lax.ppermute(value, axis, pairs)  264 us
    another operation x1, loops' own time, shards(): lax.fori_loop(0, cycle_count, cycle_step, (key_rows, value_rows, empty_kv...  162 us
    ppermute x128, waiting for transfers between devices, passed_along(): return lax.ppermute(value, axis, pairs)  85.3 us
    reduce_min x32, other arithmetic, pair_terms(): return lax.cond(jnp.max(pos_block) >= jnp.min(pos_part), live, quiet)  21.5 us
  transfers between devices with their start and end apart: 137, of which 72 were waited for; matrix products, arithmetic and copies ran while one was open for 15% of the time, Pallas kernels for 0%

commit v1 on v0

v1 whole, which is shorter than its diff:
```python
import math

import jax
import jax.numpy as jnp
from jax import lax
from jax.experimental import pallas as pl
from jax.experimental.pallas import tpu as pltpu
from jax.sharding import PartitionSpec as P

D = 128
GROUP = 8
HQ = 32
KVH = 4
TOK = 32
PLANE = 32
Q_ROWS = PLANE * TOK
PART = 256
RUN = 128
Z = 8
LOCAL = 4
QT = 256
SCALE = 1.0 / math.sqrt(D)
EXP2_SCALE = SCALE * math.log2(math.e)
BF = jnp.bfloat16
F32 = jnp.float32
MESH = pl.DeviceIdType.MESH


def pieces_of(value):
    high = value.astype(BF)
    rest = value - high.astype(F32)
    mid = rest.astype(BF)
    low = (rest - mid.astype(F32)).astype(BF)
    return high, mid, low


def kernel(
    q_ref,
    k_ref,
    v_ref,
    o_ref,
    g_ref,
    lse_ref,
    pos_ref,
    dq_out,
    dk_out,
    dv_out,
    pack0,
    pack1,
    qd,
    qt,
    gt,
    auxt,
    qpos,
    kv,
    acc,
    dqt,
    dqs,
    rs_send,
    rs,
    dq_recv,
    kv_recv,
    q_send_sem,
    q_recv_sem,
    fwd_send_sem,
    fwd_recv_sem,
    kv_send_sem,
    kv_recv_sem,
    ring_send_sem,
    ring_recv_sem,
    rs_send_sem,
    rs_recv_sem,
    dq_send_sem,
    dq_recv_sem,
    out_send_sem,
    out_recv_sem,
):
    h = lax.axis_index("head")
    b = lax.axis_index("blk")
    z = b // 4
    x_hi = (b // 2) % 2
    core = b % 2
    x_lo = h // 4
    y = h % 4
    me = (b % 4) * 8 + h
    right = (h, (b + 4) % 32)
    left = (h, (b + 28) % 32)
    sibling = (h, z * 4 + x_hi * 2 + (1 - core))

    def plane_device(p):
        return (p % 8, z * 4 + p // 8)

    barrier = pltpu.get_barrier_semaphore()

    def greet(i, carry):
        pl.semaphore_signal(
            barrier, inc=1, device_id=plane_device((me + i) % PLANE), device_id_type=MESH
        )
        return carry

    lax.fori_loop(1, PLANE, greet, 0)
    pl.semaphore_signal(barrier, inc=1, device_id=right, device_id_type=MESH)
    pl.semaphore_signal(barrier, inc=1, device_id=left, device_id_type=MESH)

    lane32 = lax.broadcasted_iota(jnp.int32, (TOK, HQ), 1)
    delta = jnp.zeros((TOK, HQ), F32)
    for head in range(HQ):
        cols = slice(head * D, (head + 1) * D)
        term = jnp.sum(
            g_ref[:, cols].astype(F32) * o_ref[:, cols].astype(F32), axis=1, keepdims=True
        )
        delta = jnp.where(lane32 == head, term, delta)
    aux_all = jnp.zeros((TOK, HQ // LOCAL * D), F32)
    sel_row = lax.broadcasted_iota(jnp.int32, (HQ, HQ // LOCAL * D), 0)
    sel_col = lax.broadcasted_iota(jnp.int32, (HQ, HQ // LOCAL * D), 1)
    sel_base = (sel_row // LOCAL) * D + 6 * (sel_row % LOCAL)
    parts = pieces_of(lse_ref[...].astype(F32) * (-math.sqrt(D))) + pieces_of(-delta)
    for index, part in enumerate(parts):
        place = jnp.where(sel_col == sel_base + index, 1.0, 0.0).astype(BF)
        aux_all = aux_all + jnp.dot(part, place, preferred_element_type=F32)
    aux_low = aux_all.astype(BF)
    for hh in range(2):
        for c in range(2):
            for g in range(4):
                slot = (hh * 2 + c) * 4 + g
                head = g * 8 + hh * 4 + 2 * c
                pack0[slot, :, 0:D] = q_ref[:, head * D : (head + 1) * D]
                pack0[slot, :, D : 2 * D] = g_ref[:, head * D : (head + 1) * D]
                pack0[slot, :, 2 * D : 3 * D] = aux_low[:, (g * 2 + hh) * D : (g * 2 + hh + 1) * D]
                pack1[slot, :, 0:D] = q_ref[:, (head + 1) * D : (head + 2) * D]
                pack1[slot, :, D : 2 * D] = g_ref[:, (head + 1) * D : (head + 2) * D]

    pl.semaphore_wait(barrier, PLANE + 1)

    key_rows = pl.ds(pl.multiple_of(x_hi * RUN + y * TOK, TOK), TOK)
    my_j = x_hi * 4 + y

    def part_device(j):
        return (x_lo * 4 + j % 4, z * 4 + (j // 4) * 2 + core)

    def kv_copy(i, which):
        j = (my_j + i) % 8
        src = (k_ref, v_ref)[which]
        cols = pl.ds(pl.multiple_of((j % 4) * D, D), D)
        return pltpu.make_async_remote_copy(
            src_ref=src.at[:, cols],
            dst_ref=kv.at[0, which, key_rows, :],
            send_sem=kv_send_sem.at[which, i],
            recv_sem=kv_recv_sem,
            device_id=part_device(j),
            device_id_type=MESH,
        )

    def kv_local(which):
        src = (k_ref, v_ref)[which]
        cols = pl.ds(pl.multiple_of(y * D, D), D)
        return pltpu.make_async_copy(src.at[:, cols], kv.at[0, which, key_rows, :], kv_recv_sem)

    def kv_start(i, carry):
        kv_copy(i, 0).start()
        kv_copy(i, 1).start()
        return carry

    lax.fori_loop(1, 8, kv_start, 0)
    kv_local(0).start()
    kv_local(1).start()

    q_rows = pl.ds(pl.multiple_of(me * TOK, TOK), TOK)

    def q_copy(stage, i):
        p = (me + i) % PLANE
        slot = (p // 8) * 4 + p % 4
        if stage == 0:
            src, dst = pack0.at[slot], qd.at[0, q_rows, :]
        else:
            src, dst = pack1.at[slot], qd.at[2, q_rows, 0 : 2 * D]
        return pltpu.make_async_remote_copy(
            src_ref=src,
            dst_ref=dst,
            send_sem=q_send_sem.at[stage, i],
            recv_sem=q_recv_sem.at[stage],
            device_id=plane_device(p),
            device_id_type=MESH,
        )

    own_slot = (me // 8) * 4 + me % 4

    def q_start(stage):
        def body(i, carry):
            q_copy(stage, i).start()
            return carry

        lax.fori_loop(1, PLANE, body, 0)

    q_start(0)
    pltpu.make_async_copy(pack0.at[own_slot], qd.at[0, q_rows, :], q_recv_sem.at[0]).start()
    q_start(1)
    pltpu.make_async_copy(
        pack1.at[own_slot], qd.at[2, q_rows, 0 : 2 * D], q_recv_sem.at[1]
    ).start()

    run_iota = lax.broadcasted_iota(jnp.int32, (1, RUN), 1)
    for r in range(8):
        qpos[0:1, r * RUN : (r + 1) * RUN] = run_iota + pos_ref[z * 4 + r // 2, (r % 2) * RUN]

    def ring_copy(src, dst, device):
        return pltpu.make_async_remote_copy(
            src_ref=kv.at[src],
            dst_ref=kv.at[dst],
            send_sem=ring_send_sem.at[dst],
            recv_sem=ring_recv_sem.at[dst],
            device_id=device,
            device_id_type=MESH,
        )

    def ring_step(i):
        @pl.when(i < 3)
        def _():
            ring_copy(i, i + 1, left).wait_recv()

            @pl.when(i < 2)
            def _():
                ring_copy(i + 1, i + 2, left).start()

        ring_copy((8 - i) % 8, 7 - i, right).wait_recv()

        @pl.when(i < 3)
        def _():
            ring_copy(7 - i, 6 - i, right).start()

    pltpu.make_async_copy(kv.at[0], kv.at[0], kv_recv_sem).wait()
    ring_copy(0, 7, right).start()
    ring_copy(0, 1, left).start()

    aux_row = lax.broadcasted_iota(jnp.int32, (D, QT), 0)
    ones = jnp.ones((2 * PART, D), BF)

    def local_head(n):
        own = core if n % 2 == 0 else 1 - core
        return 2 * own + n // 2

    def prepare(n):
        buf = n % 2
        first = 6 * local_head(n)
        for r in range(0, Q_ROWS, QT):
            cols = slice(r, r + QT)
            qt[buf, 0:D, cols] = qd[n, cols, 0:D].T
            gt[buf, 0:D, cols] = qd[n, cols, D : 2 * D].T
            if n == 0:
                auxt[:, cols] = qd[0, cols, 2 * D : 3 * D].T
            aux = auxt[:, cols]
            empty = jnp.zeros_like(aux)
            qt[buf, D : 2 * D, cols] = jnp.where(
                (aux_row >= first) & (aux_row < first + 3), aux, empty
            )
            gt[buf, D : 2 * D, cols] = jnp.where(
                (aux_row >= first + 3) & (aux_row < first + 6), aux, empty
            )
        dqt[buf] = jnp.zeros((D, Q_ROWS), F32)

    key_iota = lax.broadcasted_iota(jnp.int32, (RUN, QT), 0)

    def attend(heads, a, c):
        keys = jnp.concatenate([kv[a, 0], kv[c, 0]], axis=0)
        values = jnp.concatenate([kv[a, 1], kv[c, 1]], axis=0)
        keys_wide = jnp.concatenate([keys, ones], axis=1)
        values_wide = jnp.concatenate([values, ones], axis=1)
        keys_t = keys.T
        starts = []
        for j in range(4):
            slot = a if j < 2 else c
            row = ((z + slot) % Z) * 4 + (j % 2) * 2 + core
            starts.append(pos_ref[row, x_lo * RUN])
        dk = jnp.zeros((2 * PART, D), F32)
        dv = jnp.zeros((2 * PART, D), F32)
        for n in heads:
            buf = n % 2
            for r in range(0, Q_ROWS, QT):
                cols = slice(r, r + QT)
                scores = jnp.dot(keys_wide, qt[buf, :, cols], preferred_element_type=F32)
                shifted = jnp.dot(values_wide, gt[buf, :, cols], preferred_element_type=F32)
                raw = jnp.exp2(scores * EXP2_SCALE)
                where = qpos[0:1, cols]
                probs = jnp.concatenate(
                    [
                        jnp.where(
                            where - starts[j] >= key_iota, raw[j * RUN : (j + 1) * RUN], 0.0
                        )
                        for j in range(4)
                    ],
                    axis=0,
                )
                score_grad = (probs * shifted).astype(BF)
                dv = dv + jnp.dot(
                    probs.astype(BF), qd[n, cols, D : 2 * D], preferred_element_type=F32
                )
                dk = dk + jnp.dot(score_grad, qd[n, cols, 0:D], preferred_element_type=F32)
                dqt[buf, :, cols] += jnp.dot(keys_t, score_grad, preferred_element_type=F32)
        return dk, dv

    def slots_of(i):
        return (8 - i) % 8, i + 1

    quarter = x_lo * 2 + core

    def dq_columns(n):
        head = y * 8 + x_hi * 4 + local_head(n)
        return pl.ds(pl.multiple_of(head * D, D), D)

    def dq_copy(n, i):
        p = (me + i) % PLANE
        return pltpu.make_async_remote_copy(
            src_ref=dqs.at[n, pl.ds(pl.multiple_of(p * TOK, TOK), TOK), :],
            dst_ref=dq_recv.at[quarter, :, dq_columns(n)],
            send_sem=dq_send_sem.at[n, i],
            recv_sem=dq_recv_sem,
            device_id=plane_device(p),
            device_id_type=MESH,
        )

    def send_dq(n):
        for r in range(0, Q_ROWS, QT):
            dqs[n, r : r + QT, :] = (dqt[n % 2, :, r : r + QT] * SCALE).T.astype(BF)

        def body(i, carry):
            dq_copy(n, i).start()
            return carry

        lax.fori_loop(1, PLANE, body, 0)
        pltpu.make_async_copy(
            dqs.at[n, q_rows, :], dq_recv.at[quarter, :, dq_columns(n)], dq_recv_sem
        ).start()

    def forward(stage):
        return pltpu.make_async_remote_copy(
            src_ref=qd.at[2 * stage, :, 0 : 2 * D],
            dst_ref=qd.at[2 * stage + 1, :, 0 : 2 * D],
            send_sem=fwd_send_sem.at[stage],
            recv_sem=fwd_recv_sem.at[stage],
            device_id=sibling,
            device_id_type=MESH,
        )

    ring_step(0)
    pltpu.make_async_copy(qd.at[0], qd.at[0], q_recv_sem.at[0]).wait()
    forward(0).start()
    prepare(0)

    def first_head(i, carry):
        @pl.when(i < 3)
        def _():
            ring_step(i + 1)

        a, c = slots_of(i)
        dk, dv = attend((0,), a, c)
        acc[a, 0] = dk[:PART]
        acc[c, 0] = dk[PART:]
        acc[a, 1] = dv[:PART]
        acc[c, 1] = dv[PART:]
        return carry

    lax.fori_loop(0, 4, first_head, 0)
    send_dq(0)

    forward(0).wait_recv()
    prepare(1)

    def second_head(i, carry):
        a, c = slots_of(i)
        dk, dv = attend((1,), a, c)
        acc[a, 0] += dk[:PART]
        acc[c, 0] += dk[PART:]
        acc[a, 1] += dv[:PART]
        acc[c, 1] += dv[PART:]
        return carry

    lax.fori_loop(0, 4, second_head, 0)
    send_dq(1)

    pltpu.make_async_copy(
        qd.at[2, :, 0 : 2 * D], qd.at[2, :, 0 : 2 * D], q_recv_sem.at[1]
    ).wait()
    forward(1).start()
    prepare(2)
    forward(1).wait_recv()
    prepare(3)

    def rs_copy(src, dst, device):
        return pltpu.make_async_remote_copy(
            src_ref=rs_send.at[src],
            dst_ref=rs.at[dst],
            send_sem=rs_send_sem.at[dst],
            recv_sem=rs_recv_sem.at[dst],
            device_id=device,
            device_id_type=MESH,
        )

    def last_heads(step, carry):
        i = 3 - step
        a, c = slots_of(i)
        dk, dv = attend((2, 3), a, c)
        acc[a, 0] += dk[:PART]
        acc[c, 0] += dk[PART:]
        acc[a, 1] += dv[:PART]
        acc[c, 1] += dv[PART:]

        @pl.when(step > 0)
        def _():
            rs_copy(c + 1, c, right).wait_recv()
            acc[c] += rs[c].astype(F32)

        rs_send[c] = acc[c].astype(BF)
        rs_copy(c, c - 1, right).start()

        @pl.when((step > 0) & (step < 3))
        def _():
            rs_copy(a - 1, a, left).wait_recv()
            acc[a] += rs[a].astype(F32)

        @pl.when(step < 2)
        def _():
            rs_send[a] = acc[a].astype(BF)
            rs_copy(a, a + 1, left).start()

        @pl.when(step == 2)
        def _():
            rs_send[7] = acc[7].astype(BF)
            rs_copy(7, 4, left).start()

        return carry

    lax.fori_loop(0, 4, last_heads, 0)
    send_dq(2)
    send_dq(3)

    rs_copy(7, 4, left).wait_recv()
    rs_copy(1, 0, right).wait_recv()
    rs_send[0] = (acc[0] + rs[4].astype(F32) + rs[0].astype(F32)).astype(BF)

    out_cols = pl.ds(pl.multiple_of(y * D, D), D)

    def out_copy(i, which):
        j = (my_j + i) % 8
        rows = pl.ds(pl.multiple_of((j // 4) * RUN + (j % 4) * TOK, TOK), TOK)
        return pltpu.make_async_remote_copy(
            src_ref=rs_send.at[0, which, rows, :],
            dst_ref=kv_recv.at[x_hi, which, :, out_cols],
            send_sem=out_send_sem.at[which, i],
            recv_sem=out_recv_sem,
            device_id=part_device(j),
            device_id_type=MESH,
        )

    def out_start(i, carry):
        out_copy(i, 0).start()
        out_copy(i, 1).start()
        return carry

    lax.fori_loop(1, 8, out_start, 0)
    for which in range(2):
        pltpu.make_async_copy(
            rs_send.at[0, which, key_rows, :], kv_recv.at[x_hi, which, :, out_cols], out_recv_sem
        ).start()

    pltpu.make_async_copy(dq_recv, dq_recv, dq_recv_sem).wait()
    for r in range(0, HQ * D, 512):
        cols = slice(r, r + 512)
        total = dq_recv[0, :, cols].astype(F32) + dq_recv[1, :, cols].astype(F32)
        total = total + dq_recv[2, :, cols].astype(F32) + dq_recv[3, :, cols].astype(F32)
        dq_out[:, cols] = total.astype(BF)
    pltpu.make_async_copy(kv_recv, kv_recv, out_recv_sem).wait()
    dk_out[...] = ((kv_recv[0, 0].astype(F32) + kv_recv[1, 0].astype(F32)) * SCALE).astype(BF)
    dv_out[...] = (kv_recv[0, 1].astype(F32) + kv_recv[1, 1].astype(F32)).astype(BF)

    def finish_plane(i, carry):
        q_copy(0, i).wait_send()
        q_copy(1, i).wait_send()
        for n in range(LOCAL):
            dq_copy(n, i).wait_send()
        return carry

    lax.fori_loop(1, PLANE, finish_plane, 0)

    def finish_part(i, carry):
        for which in range(2):
            kv_copy(i, which).wait_send()
            out_copy(i, which).wait_send()
        return carry

    lax.fori_loop(1, 8, finish_part, 0)
    forward(0).wait_send()
    forward(1).wait_send()
    for dst in range(1, 8):
        ring_copy(0, dst, right).wait_send()
    for dst in (0, 1, 2, 3, 4, 6, 7):
        rs_copy(0, dst, right).wait_send()


def shards(queries, key_heads, value_heads, outputs, out_grad, log_total, positions):
    vmem = pl.BlockSpec(memory_space=pltpu.VMEM)
    smem = pl.BlockSpec(memory_space=pltpu.SMEM)
    dma = pltpu.SemaphoreType.DMA
    return pl.pallas_call(
        kernel,
        out_shape=(
            jax.ShapeDtypeStruct((TOK, HQ * D), BF),
            jax.ShapeDtypeStruct((TOK, KVH * D), BF),
            jax.ShapeDtypeStruct((TOK, KVH * D), BF),
        ),
        in_specs=[vmem] * 6 + [smem],
        out_specs=(vmem, vmem, vmem),
        scratch_shapes=[
            pltpu.VMEM((16, TOK, 3 * D), BF),
            pltpu.VMEM((16, TOK, 2 * D), BF),
            pltpu.VMEM((LOCAL, Q_ROWS, 3 * D), BF),
            pltpu.VMEM((2, 2 * D, Q_ROWS), BF),
            pltpu.VMEM((2, 2 * D, Q_ROWS), BF),
            pltpu.VMEM((D, Q_ROWS), BF),
            pltpu.VMEM((8, Q_ROWS), jnp.int32),
            pltpu.VMEM((Z, 2, PART, D), BF),
            pltpu.VMEM((Z, 2, PART, D), F32),
            pltpu.VMEM((2, D, Q_ROWS), F32),
            pltpu.VMEM((LOCAL, Q_ROWS, D), BF),
            pltpu.VMEM((Z, 2, PART, D), BF),
            pltpu.VMEM((Z, 2, PART, D), BF),
            pltpu.VMEM((4, TOK, HQ * D), BF),
            pltpu.VMEM((2, 2, TOK, KVH * D), BF),
            dma((2, PLANE)),
            dma((2,)),
            dma((2,)),
            dma((2,)),
            dma((2, 8)),
            dma,
            dma((Z,)),
            dma((Z,)),
            dma((Z,)),
            dma((Z,)),
            dma((LOCAL, PLANE)),
            dma,
            dma((2, 8)),
            dma,
        ],
        compiler_params=pltpu.CompilerParams(
            collective_id=0, has_side_effects=True, vmem_limit_bytes=50 << 20
        ),
    )(queries, key_heads, value_heads, outputs, out_grad, log_total, positions)


def solution(mesh):
    spec = P(("head", "blk"), None)
    return jax.shard_map(
        shards,
        mesh=mesh,
        in_specs=(spec,) * 6 + (P(),),
        out_specs=(spec,) * 3,
        check_vma=False,
    )
```

time: 716 us -> 91.4 us (0.13); the launches traced: 706 us -> 91 us
  starting transfers between devices: 297 us -> 0 us
  loops' own time: 168 us -> 0 us
  waiting for transfers between devices: 128 us -> 0 us
  Pallas kernels: 0 us -> 82.6 us
  matrix products: 57.4 us -> 0 us
  other arithmetic: 38.2 us -> 0 us
  local copies, waits for them, and re-layouts: 16.1 us -> 7.74 us
    ppermute x128 -> x0, starting transfers between devices: 264 us -> none  [passed_along(): return lax.ppermute(value, axis, pairs)]
    another operation x129 -> x0, loops' own time: 168 us -> none  [the longest x1 162 us: shards(): lax.fori_loop(0, cycle_count, cycle_step, (key_rows, value_rows, empty_kv...]
    ppermute x128 -> x0, waiting for transfers between devices: 85.3 us -> none  [passed_along(): return lax.ppermute(value, axis, pairs)]
    pallas_call x0 -> x1, Pallas kernels: none -> 82.6 us  [shards(): pl.pallas_call(kernel, out_shape=(jax.ShapeDtypeStruct((TOK, HQ * D), BF)...]
    dot_general x280 -> x0, matrix products: 57.4 us -> none  [the longest x56 12.7 us: live(): jnp.einsum('qhk,qhd->kd', probs.astype(jnp.bfloat16), grad_block, preferr...]
    all_to_all x9 -> x0, waiting for transfers between devices: 42.9 us -> none  [the longest x1 5.76 us: shards(): lax.all_to_all(out_grad, 'head', split_axis=1, concat_axis=0, tiled=True)]
    all_to_all x9 -> x0, starting transfers between devices: 33.4 us -> none  [the longest x1 5.95 us: shards(): lax.all_to_all(log_total, 'head', split_axis=1, concat_axis=0, tiled=True)]
    reduce_min x32 -> x0, other arithmetic: 21.5 us -> none  [pair_terms(): return lax.cond(jnp.max(pos_block) >= jnp.min(pos_part), live, quiet)]
  transfers between devices with their start and end apart: 137 -> 0, of which waited for: 72 -> 0; matrix products, arithmetic and copies ran while one was open for 15% -> 0% of each run, Pallas kernels for 0% -> 0%
where the time goes in v1:
time: 91.4 us; the launch traced here: 91 us
  Pallas kernels  82.6 us (90%)
  local copies, waits for them, and re-layouts  7.74 us (8%)
    pallas_call x1, Pallas kernels, shards(): pl.pallas_call(kernel, out_shape=(jax.ShapeDtypeStruct((TOK, HQ * D), BF)...  82.6 us
    unnamed x17, local copies, waits for them, and re-layouts  7.74 us

profile of v1, /device:TPU:1, one launch (start us, length us, event | category | flops | bytes accessed | tf_op | source)
XLA Modules:
  0.0 91.0 jit_solution(2726362494565579223)
XLA Ops:
  0.6 0.0 copy-start
  0.6 0.9 %copy-done = bf16[32,4096]{1,0:T(8,128)(2,1)S(1)} copy-done((bf16[32,4096]{1,0:T(8,128)(2,1)S(1)}, bf16[32,4096]{1,0:T(8,128)(2,1)}, u32[]{:S(2)}) %copy-start) | copy-done | bytes 262168
  1.6 0.0 copy-start.1
  1.6 0.9 %copy-done.1 = bf16[32,4096]{1,0:T(8,128)(2,1)S(1)} copy-done((bf16[32,4096]{1,0:T(8,128)(2,1)S(1)}, bf16[32,4096]{1,0:T(8,128)(2,1)}, u32[]{:S(2)}) %copy-start.1) | copy-done | bytes 262168
  2.5 0.0 copy-start.2
  2.5 0.9 %copy-done.2 = bf16[32,4096]{1,0:T(8,128)(2,1)S(1)} copy-done((bf16[32,4096]{1,0:T(8,128)(2,1)S(1)}, bf16[32,4096]{1,0:T(8,128)(2,1)}, u32[]{:S(2)}) %copy-start.2) | copy-done | bytes 262168
  3.5 0.0 copy-start.3
  3.5 0.8 copy-done.3
  4.2 0.0 copy-start.4
  4.2 0.8 copy-done.4
  5.0 0.0 copy-start.5
  5.0 0.8 copy-done.5
  5.8 0.0 copy-start.6
  5.8 0.7 copy-done.6
  6.5 82.6 %shard_map.94 = (bf16[32,4096]{1,0:T(8,128)(2,1)S(1)}, bf16[32,512]{1,0:T(8,128)(2,1)S(1)}, bf16[32,512]{1,0:T(8,128)(2,1)S(1)}) custom-call(bf16[32,4096]{1,0:T(8,128)(2,1)S(1)} %copy-done, bf16[32,512]{1,0:T(8,128)(2,1)S(1)} %copy-done.3, bf16[32,512]{1,0:T(8,128)(2,1)S(1)} %copy-done.4, bf16[32,4096]{1,0:T(8,128)(2,1)S(1)} %copy-done.1, ...), custom_call_target="tpu_custom_call" | custom-call | tf_op jit(solution)/shard_map/pallas_call | solution.py:503
  89.0 0.7 copy.13
  89.7 0.6 copy.14
  90.3 0.6 copy.15
Async XLA Ops:
  0.6 1.0 %copy-start = (bf16[32,4096]{1,0:T(8,128)(2,1)S(1)}, bf16[32,4096]{1,0:T(8,128)(2,1)}, u32[]{:S(2)}) copy-start(bf16[32,4096]{1,0:T(8,128)(2,1)} %q_ref.1) | copy-start | bytes 786436
  1.6 0.9 %copy-start.1 = (bf16[32,4096]{1,0:T(8,128)(2,1)S(1)}, bf16[32,4096]{1,0:T(8,128)(2,1)}, u32[]{:S(2)}) copy-start(bf16[32,4096]{1,0:T(8,128)(2,1)} %o_ref.1) | copy-start | bytes 786436
  2.5 0.9 %copy-start.2 = (bf16[32,4096]{1,0:T(8,128)(2,1)S(1)}, bf16[32,4096]{1,0:T(8,128)(2,1)}, u32[]{:S(2)}) copy-start(bf16[32,4096]{1,0:T(8,128)(2,1)} %g_ref.1) | copy-start | bytes 786436
  3.5 0.8 copy-start.3
  4.2 0.8 copy-start.4
  5.0 0.8 copy-start.5
  5.8 0.7 copy-start.6

commit v2 on v1

v2 whole, which is shorter than its diff:
```python
import math

import jax
import jax.numpy as jnp
from jax import lax
from jax.experimental import pallas as pl
from jax.experimental.pallas import tpu as pltpu
from jax.sharding import PartitionSpec as P

D = 128
HQ = 32
KVH = 4
TOK = 32
SUB = TOK // 2
PLANE = 32
HALF = PLANE * SUB
Q_ROWS = 2 * HALF
PART = 256
RUN = 128
Z = 8
LOCAL = 4
QT = 256
SCALE = 1.0 / math.sqrt(D)
EXP2_SCALE = SCALE * math.log2(math.e)
BF = jnp.bfloat16
F32 = jnp.float32
MESH = pl.DeviceIdType.MESH


def pieces_of(value):
    high = value.astype(BF)
    rest = value - high.astype(F32)
    mid = rest.astype(BF)
    low = (rest - mid.astype(F32)).astype(BF)
    return high, mid, low


def kernel(
    q_hbm,
    k_hbm,
    v_hbm,
    o_hbm,
    g_hbm,
    lse_hbm,
    pos_hbm,
    dq_out,
    dk_out,
    dv_out,
    q_ref,
    k_ref,
    v_ref,
    o_ref,
    g_ref,
    lse_ref,
    pos_ref,
    pack,
    pack_aux,
    qd,
    aux,
    auxt,
    qt,
    gt,
    qpos,
    kv,
    acc,
    dqt,
    dqs,
    dqx_send,
    dqx,
    rs_send,
    rs,
    dq_recv,
    kv_recv,
    in_sem,
    q_send_sem,
    q_recv_sem,
    fwd_send_sem,
    fwd_recv_sem,
    kv_send_sem,
    kv_recv_sem,
    ring_send_sem,
    ring_recv_sem,
    rs_send_sem,
    rs_recv_sem,
    dqx_send_sem,
    dqx_recv_sem,
    dq_send_sem,
    dq_recv_sem,
    out_send_sem,
    out_recv_sem,
):
    loads = [
        pltpu.make_async_copy(src, dst, in_sem.at[index])
        for index, (src, dst) in enumerate(
            [
                (g_hbm, g_ref),
                (o_hbm, o_ref),
                (lse_hbm, lse_ref),
                (q_hbm, q_ref),
                (k_hbm, k_ref),
                (v_hbm, v_ref),
                (pos_hbm, pos_ref),
            ]
        )
    ]
    for load in loads:
        load.start()

    h = lax.axis_index("head")
    b = lax.axis_index("blk")
    z = b // 4
    x_hi = (b // 2) % 2
    core = b % 2
    x_lo = h // 4
    y = h % 4
    me = (b % 4) * 8 + h
    right = (h, (b + 4) % 32)
    left = (h, (b + 28) % 32)
    sibling = (h, z * 4 + x_hi * 2 + (1 - core))

    def plane_device(p):
        return (p % 8, z * 4 + p // 8)

    barrier = pltpu.get_barrier_semaphore()

    def greet(i, carry):
        pl.semaphore_signal(
            barrier, inc=1, device_id=plane_device((me + i) % PLANE), device_id_type=MESH
        )
        return carry

    lax.fori_loop(1, PLANE, greet, 0)
    pl.semaphore_signal(barrier, inc=1, device_id=right, device_id_type=MESH)
    pl.semaphore_signal(barrier, inc=1, device_id=left, device_id_type=MESH)

    groups = HQ // LOCAL
    sel_row = lax.broadcasted_iota(jnp.int32, (HQ, groups * D), 0)
    sel_col = lax.broadcasted_iota(jnp.int32, (HQ, groups * D), 1)
    sel_rel = sel_col - ((sel_row // LOCAL) * D + 6 * (sel_row % LOCAL))
    lane32 = lax.broadcasted_iota(jnp.int32, (TOK, HQ), 1)
    delta = jnp.zeros((TOK, HQ), F32)
    for load in loads[:3]:
        load.wait()
    for head in range(HQ):
        cols = slice(head * D, (head + 1) * D)
        term = jnp.sum(
            g_ref[:, cols].astype(F32) * o_ref[:, cols].astype(F32), axis=1, keepdims=True
        )
        delta = jnp.where(lane32 == head, term, delta)
    aux_sum = jnp.zeros((SUB, groups * D), F32)
    parts = pieces_of(lse_ref[...].astype(F32) * (-math.sqrt(D))) + pieces_of(-delta)
    for index, part in enumerate(parts):
        for t in range(2):
            place = jnp.where(sel_rel == 32 * t + index, 1.0, 0.0).astype(BF)
            aux_sum = aux_sum + jnp.dot(
                part[t * SUB : (t + 1) * SUB], place, preferred_element_type=F32
            )
    aux_low = aux_sum.astype(BF)
    for group in range(groups):
        pack_aux[group] = aux_low[:, group * D : (group + 1) * D]
    for load in loads[3:]:
        load.wait()
    for hh in range(2):
        for c in range(2):
            for g in range(4):
                for j in range(2):
                    head = g * 8 + hh * 4 + 2 * c + j
                    cols = slice(head * D, (head + 1) * D)
                    slot = (hh * 2 + c) * 4 + g
                    for t in range(2):
                        rows = slice(t * SUB, (t + 1) * SUB)
                        pack[slot, j, t, 0:SUB, :] = q_ref[rows, cols]
                        pack[slot, j, t, SUB : 2 * SUB, :] = g_ref[rows, cols]

    pl.semaphore_wait(barrier, PLANE + 1)

    key_rows = pl.ds(pl.multiple_of(x_hi * RUN + y * TOK, TOK), TOK)
    my_j = x_hi * 4 + y

    def part_device(j):
        return (x_lo * 4 + j % 4, z * 4 + (j // 4) * 2 + core)

    def kv_copy(i, which):
        j = (my_j + i) % 8
        src = (k_ref, v_ref)[which]
        cols = pl.ds(pl.multiple_of((j % 4) * D, D), D)
        return pltpu.make_async_remote_copy(
            src_ref=src.at[:, cols],
            dst_ref=kv.at[0, which, key_rows, :],
            send_sem=kv_send_sem.at[which, i],
            recv_sem=kv_recv_sem.at[which],
            device_id=part_device(j),
            device_id_type=MESH,
        )

    own_cols = pl.ds(pl.multiple_of(y * D, D), D)
    for which in range(2):

        def kv_start(i, carry, which=which):
            kv_copy(i, which).start()
            return carry

        lax.fori_loop(1, 8, kv_start, 0)
        pltpu.make_async_copy(
            (k_ref, v_ref)[which].at[:, own_cols],
            kv.at[0, which, key_rows, :],
            kv_recv_sem.at[which],
        ).start()

    def q_ends(stage, p):
        slot = (p // 8) * 4 + p % 4
        if stage < 2:
            return pack.at[slot, 0, stage], qd.at[0, stage, me]
        if stage == 2:
            return pack.at[slot, 1], qd.at[2, :, me]
        return pack_aux.at[(p % 4) * 2 + p // 16], aux.at[me]

    def q_copy(stage, i):
        p = (me + i) % PLANE
        src, dst = q_ends(stage, p)
        return pltpu.make_async_remote_copy(
            src_ref=src,
            dst_ref=dst,
            send_sem=q_send_sem.at[stage, i],
            recv_sem=q_recv_sem.at[stage],
            device_id=plane_device(p),
            device_id_type=MESH,
        )

    def q_start(stages):
        def body(i, carry):
            for stage in stages:
                q_copy(stage, i).start()
            return carry

        lax.fori_loop(1, PLANE, body, 0)
        for stage in stages:
            src, dst = q_ends(stage, me)
            pltpu.make_async_copy(src, dst, q_recv_sem.at[stage]).start()

    def all_of(ref, sem):
        pltpu.make_async_copy(ref, ref, sem).wait()

    def ring_copy(src, dst, which, device):
        return pltpu.make_async_remote_copy(
            src_ref=kv.at[src, which],
            dst_ref=kv.at[dst, which],
            send_sem=ring_send_sem.at[which, dst],
            recv_sem=ring_recv_sem.at[which, dst],
            device_id=device,
            device_id_type=MESH,
        )

    def ring_step(i):
        for which in range(2):
            ring_copy(0, 7 - i, which, right).wait_recv()

            @pl.when(i < 3)
            def _(which=which):
                ring_copy(7 - i, 6 - i, which, right).start()
                ring_copy(0, 1 + i, which, left).wait_recv()

            @pl.when(i < 2)
            def _(which=which):
                ring_copy(1 + i, 2 + i, which, left).start()

    q_start((0, 3))
    for which in range(2):
        all_of(kv.at[0, which], kv_recv_sem.at[which])
        ring_copy(0, 7, which, right).start()
        ring_copy(0, 1, which, left).start()
    q_start((1,))
    q_start((2,))

    lane = lax.broadcasted_iota(jnp.int32, (1, HALF), 1)
    run_of = lax.shift_right_logical(lane, 6)
    inside = lax.shift_right_logical(lane, 4) % 4 * TOK + lane % SUB
    run_start = jnp.zeros((1, HALF), jnp.int32)
    for r in range(8):
        run_start = jnp.where(
            run_of == r, pos_ref[z * 4 + r // 2, (r % 2) * RUN], run_start
        )
    for t in range(2):
        qpos[0:1, t * HALF : (t + 1) * HALF] = run_start + inside + t * SUB
    acc[...] = jnp.zeros_like(acc)
    dqt[...] = jnp.zeros_like(dqt)

    aux_row = lax.broadcasted_iota(jnp.int32, (D, HALF), 0)
    ones = jnp.ones((2 * PART, D), BF)

    def local_head(n):
        own = core if n % 2 == 0 else 1 - core
        return 2 * own + n // 2

    def queries_of(n, t, r):
        first = r // SUB
        return qd[n, t, first : first + QT // SUB, 0:SUB, :].reshape(QT, D)

    def cotangents_of(n, t, r):
        first = r // SUB
        return qd[n, t, first : first + QT // SUB, SUB : 2 * SUB, :].reshape(QT, D)

    def prepare(n, t):
        for r in range(0, HALF, QT):
            cols = slice(t * HALF + r, t * HALF + r + QT)
            qt[n, 0:D, cols] = queries_of(n, t, r).T
            gt[n, 0:D, cols] = cotangents_of(n, t, r).T
        first = 32 * t + 6 * local_head(n)
        cols = slice(t * HALF, (t + 1) * HALF)
        every = auxt[...]
        empty = jnp.zeros_like(every)
        qt[n, D : 2 * D, cols] = jnp.where(
            (aux_row >= first) & (aux_row < first + 3), every, empty
        )
        gt[n, D : 2 * D, cols] = jnp.where(
            (aux_row >= first + 3) & (aux_row < first + 6), every, empty
        )

    key_iota = lax.broadcasted_iota(jnp.int32, (RUN, QT), 0)

    def attend(heads, halves, a, c):
        keys = jnp.concatenate([kv[a, 0], kv[c, 0]], axis=0)
        values = jnp.concatenate([kv[a, 1], kv[c, 1]], axis=0)
        keys_wide = jnp.concatenate([keys, ones], axis=1)
        values_wide = jnp.concatenate([values, ones], axis=1)
        keys_t = keys.T
        starts = []
        for j in range(4):
            slot = a if j < 2 else c
            row = ((z + slot) % Z) * 4 + (j % 2) * 2 + core
            starts.append(pos_ref[row, x_lo * RUN])
        dk = jnp.zeros((2 * PART, D), F32)
        dv = jnp.zeros((2 * PART, D), F32)
        for n in heads:
            for t in halves:
                for r in range(0, HALF, QT):
                    cols = slice(t * HALF + r, t * HALF + r + QT)
                    scores = jnp.dot(keys_wide, qt[n, :, cols], preferred_element_type=F32)
                    shifted = jnp.dot(values_wide, gt[n, :, cols], preferred_element_type=F32)
                    raw = jnp.exp2(scores * EXP2_SCALE)
                    where = qpos[0:1, cols]
                    probs = jnp.concatenate(
                        [
                            jnp.where(
                                where - starts[j] >= key_iota, raw[j * RUN : (j + 1) * RUN], 0.0
                            )
                            for j in range(4)
                        ],
                        axis=0,
                    )
                    score_grad = (probs * shifted).astype(BF)
                    dv = dv + jnp.dot(
                        probs.astype(BF), cotangents_of(n, t, r), preferred_element_type=F32
                    )
                    dk = dk + jnp.dot(
                        score_grad, queries_of(n, t, r), preferred_element_type=F32
                    )
                    dqt[n, :, cols] += jnp.dot(
                        keys_t, score_grad, preferred_element_type=F32
                    )
        acc[a, 0] += dk[:PART]
        acc[c, 0] += dk[PART:]
        acc[a, 1] += dv[:PART]
        acc[c, 1] += dv[PART:]

    def slots_of(i):
        return 7 - i, (1 + i) % 4

    def swap(k):
        return pltpu.make_async_remote_copy(
            src_ref=dqx_send.at[k],
            dst_ref=dqx.at[k],
            send_sem=dqx_send_sem.at[k],
            recv_sem=dqx_recv_sem.at[k],
            device_id=sibling,
            device_id_type=MESH,
        )

    def swap_start(k):
        for r in range(0, Q_ROWS, QT):
            dqx_send[k, r : r + QT, :] = (dqt[2 * k + 1, :, r : r + QT] * SCALE).T.astype(BF)
        swap(k).start()

    def dq_columns(k):
        head = y * 8 + x_hi * 4 + 2 * core + k
        return pl.ds(pl.multiple_of(head * D, D), D)

    def dq_copy(k, i):
        p = (me + i) % PLANE
        return pltpu.make_async_remote_copy(
            src_ref=dqs.at[k, :, p],
            dst_ref=dq_recv.at[x_lo, :, :, dq_columns(k)],
            send_sem=dq_send_sem.at[k, i],
            recv_sem=dq_recv_sem,
            device_id=plane_device(p),
            device_id_type=MESH,
        )

    def send_dq(k):
        swap(k).wait_recv()
        for r in range(0, Q_ROWS, QT):
            total = (dqt[2 * k, :, r : r + QT] * SCALE).T + dqx[k, r : r + QT, :].astype(F32)
            first = (r % HALF) // SUB
            dqs[k, r // HALF, first : first + QT // SUB] = total.astype(BF).reshape(
                QT // SUB, SUB, D
            )

        def body(i, carry):
            dq_copy(k, i).start()
            return carry

        lax.fori_loop(1, PLANE, body, 0)
        pltpu.make_async_copy(
            dqs.at[k, :, me], dq_recv.at[x_lo, :, :, dq_columns(k)], dq_recv_sem
        ).start()

    def forward(stage):
        src = qd.at[0, stage] if stage < 2 else qd.at[2]
        dst = qd.at[1, stage] if stage < 2 else qd.at[3]
        return pltpu.make_async_remote_copy(
            src_ref=src,
            dst_ref=dst,
            send_sem=fwd_send_sem.at[stage],
            recv_sem=fwd_recv_sem.at[stage],
            device_id=sibling,
            device_id_type=MESH,
        )

    all_of(qd.at[0, 0], q_recv_sem.at[0])
    forward(0).start()
    all_of(aux, q_recv_sem.at[3])
    auxt[...] = aux[...].reshape(HALF, D).T
    prepare(0, 0)
    ring_step(0)
    forward(0).wait_recv()
    prepare(1, 0)
    attend((0, 1), (0,), 7, 1)
    all_of(qd.at[0, 1], q_recv_sem.at[1])
    forward(1).start()
    prepare(0, 1)
    forward(1).wait_recv()
    prepare(1, 1)
    attend((0, 1), (1,), 7, 1)

    def first_heads(i, carry):
        ring_step(i)
        a, c = slots_of(i)
        attend((0, 1), (0, 1), a, c)
        return carry

    lax.fori_loop(1, 4, first_heads, 0)
    swap_start(0)

    all_of(qd.at[2], q_recv_sem.at[2])
    forward(2).start()
    prepare(2, 0)
    prepare(2, 1)
    send_dq(0)
    forward(2).wait_recv()
    prepare(3, 0)
    prepare(3, 1)

    def rs_copy(src, dst, which, device):
        return pltpu.make_async_remote_copy(
            src_ref=rs_send.at[src, which],
            dst_ref=rs.at[dst, which],
            send_sem=rs_send_sem.at[which, dst],
            recv_sem=rs_recv_sem.at[which, dst],
            device_id=device,
            device_id_type=MESH,
        )

    def last_heads(step, carry):
        a, c = slots_of(3 - step)
        attend((2, 3), (0, 1), a, c)
        down = 4 - step
        up = 4 + step
        for which in range(2):

            @pl.when(step > 0)
            def _(which=which):
                rs_copy(0, down, which, right).wait_recv()
                acc[down, which] += rs[down, which].astype(F32)

            rs_send[down, which] = acc[down, which].astype(BF)
            rs_copy(down, down - 1, which, right).start()

            @pl.when(step > 1)
            def _(which=which):
                rs_copy(0, up, which, left).wait_recv()
                acc[up, which] += rs[up, which].astype(F32)

            @pl.when(step > 0)
            def _(which=which):
                rs_send[up, which] = acc[up, which].astype(BF)
                rs_copy(up, up + 1 - 4 * (up // 7), which, left).start()

        return carry

    lax.fori_loop(0, 4, last_heads, 0)
    swap_start(1)
    send_dq(1)

    def out_copy(i, which):
        j = (my_j + i) % 8
        rows = pl.ds(pl.multiple_of((j // 4) * RUN + (j % 4) * TOK, TOK), TOK)
        return pltpu.make_async_remote_copy(
            src_ref=rs_send.at[0, which, rows, :],
            dst_ref=kv_recv.at[x_hi, which, :, own_cols],
            send_sem=out_send_sem.at[which, i],
            recv_sem=out_recv_sem,
            device_id=part_device(j),
            device_id_type=MESH,
        )

    for which in range(2):
        rs_copy(0, 4, which, left).wait_recv()
        rs_copy(0, 0, which, right).wait_recv()
        rs_send[0, which] = (
            acc[0, which] + rs[4, which].astype(F32) + rs[0, which].astype(F32)
        ).astype(BF)

        def out_start(i, carry, which=which):
            out_copy(i, which).start()
            return carry

        lax.fori_loop(1, 8, out_start, 0)
        pltpu.make_async_copy(
            rs_send.at[0, which, key_rows, :], kv_recv.at[x_hi, which, :, own_cols], out_recv_sem
        ).start()

    all_of(dq_recv, dq_recv_sem)
    for t in range(2):
        for r in range(0, HQ * D, 512):
            cols = slice(r, r + 512)
            total = dq_recv[0, t, :, cols].astype(F32) + dq_recv[1, t, :, cols].astype(F32)
            dq_out[t * SUB : (t + 1) * SUB, cols] = total.astype(BF)
    all_of(kv_recv, out_recv_sem)
    dk_out[...] = ((kv_recv[0, 0].astype(F32) + kv_recv[1, 0].astype(F32)) * SCALE).astype(BF)
    dv_out[...] = (kv_recv[0, 1].astype(F32) + kv_recv[1, 1].astype(F32)).astype(BF)

    def finish_plane(i, carry):
        for stage in range(4):
            q_copy(stage, i).wait_send()
        for k in range(2):
            dq_copy(k, i).wait_send()
        return carry

    lax.fori_loop(1, PLANE, finish_plane, 0)

    def finish_part(i, carry):
        for which in range(2):
            kv_copy(i, which).wait_send()
            out_copy(i, which).wait_send()
        return carry

    lax.fori_loop(1, 8, finish_part, 0)
    for stage in range(3):
        forward(stage).wait_send()
    for k in range(2):
        swap(k).wait_send()
    for which in range(2):
        for dst in range(1, 8):
            ring_copy(0, dst, which, right).wait_send()
        for dst in (0, 1, 2, 3, 4, 6, 7):
            rs_copy(0, dst, which, right).wait_send()


def shards(queries, key_heads, value_heads, outputs, out_grad, log_total, positions):
    vmem = pl.BlockSpec(memory_space=pltpu.VMEM)
    anywhere = pl.BlockSpec(memory_space=pl.ANY)
    dma = pltpu.SemaphoreType.DMA
    return pl.pallas_call(
        kernel,
        out_shape=(
            jax.ShapeDtypeStruct((TOK, HQ * D), BF),
            jax.ShapeDtypeStruct((TOK, KVH * D), BF),
            jax.ShapeDtypeStruct((TOK, KVH * D), BF),
        ),
        in_specs=[anywhere] * 7,
        out_specs=(vmem, vmem, vmem),
        scratch_shapes=[
            pltpu.VMEM((TOK, HQ * D), BF),
            pltpu.VMEM((TOK, KVH * D), BF),
            pltpu.VMEM((TOK, KVH * D), BF),
            pltpu.VMEM((TOK, HQ * D), BF),
            pltpu.VMEM((TOK, HQ * D), BF),
            pltpu.VMEM((TOK, HQ), BF),
            pltpu.SMEM((32, 256), jnp.int32),
            pltpu.VMEM((16, 2, 2, 2 * SUB, D), BF),
            pltpu.VMEM((8, SUB, D), BF),
            pltpu.VMEM((LOCAL, 2, PLANE, 2 * SUB, D), BF),
            pltpu.VMEM((PLANE, SUB, D), BF),
            pltpu.VMEM((D, HALF), BF),
            pltpu.VMEM((LOCAL, 2 * D, Q_ROWS), BF),
            pltpu.VMEM((LOCAL, 2 * D, Q_ROWS), BF),
            pltpu.VMEM((8, Q_ROWS), jnp.int32),
            pltpu.VMEM((Z, 2, PART, D), BF),
            pltpu.VMEM((Z, 2, PART, D), F32),
            pltpu.VMEM((LOCAL, D, Q_ROWS), F32),
            pltpu.VMEM((2, 2, PLANE, SUB, D), BF),
            pltpu.VMEM((2, Q_ROWS, D), BF),
            pltpu.VMEM((2, Q_ROWS, D), BF),
            pltpu.VMEM((Z, 2, PART, D), BF),
            pltpu.VMEM((Z, 2, PART, D), BF),
            pltpu.VMEM((2, 2, SUB, HQ * D), BF),
            pltpu.VMEM((2, 2, TOK, KVH * D), BF),
            dma((7,)),
            dma((4, PLANE)),
            dma((4,)),
            dma((3,)),
            dma((3,)),
            dma((2, 8)),
            dma((2,)),
            dma((2, Z)),
            dma((2, Z)),
            dma((2, Z)),
            dma((2, Z)),
            dma((2,)),
            dma((2,)),
            dma((2, PLANE)),
            dma,
            dma((2, 8)),
            dma,
        ],
        compiler_params=pltpu.CompilerParams(
            collective_id=0, has_side_effects=True, vmem_limit_bytes=60 << 20
        ),
    )(queries, key_heads, value_heads, outputs, out_grad, log_total, positions)


def solution(mesh):
    spec = P(("head", "blk"), None)
    return jax.shard_map(
        shards,
        mesh=mesh,
        in_specs=(spec,) * 6 + (P(),),
        out_specs=(spec,) * 3,
        check_vma=False,
    )
```

time: 91.4 us -> 73.4 us (0.80)
  Pallas kernels: 82.6 us -> 69.5 us
  local copies, waits for them, and re-layouts: 7.74 us -> 3.06 us
    pallas_call x1, Pallas kernels: 82.6 us -> 69.5 us  [shards(): pl.pallas_call(kernel, out_shape=(jax.ShapeDtypeStruct((TOK, HQ * D), BF)...]
    unnamed x17 -> x7, local copies, waits for them, and re-layouts: 7.74 us -> 3.06 us
where the time goes in v2:
time: 73.4 us; the launch traced here: 73.2 us
  Pallas kernels  69.5 us (95%)
  local copies, waits for them, and re-layouts  3.06 us (4%)
    pallas_call x1, Pallas kernels, shards(): pl.pallas_call(kernel, out_shape=(jax.ShapeDtypeStruct((TOK, HQ * D), BF)...  69.5 us
    unnamed x7, local copies, waits for them, and re-layouts  3.06 us

profile of v2, /device:TPU:1, one launch (start us, length us, event | category | flops | bytes accessed | tf_op | source)
XLA Modules:
  0.0 73.2 jit_solution(9827007899995558366)
XLA Ops:
  0.6 69.5 %shard_map.94 = (bf16[32,4096]{1,0:T(8,128)(2,1)}, bf16[32,512]{1,0:T(8,128)(2,1)}, bf16[32,512]{1,0:T(8,128)(2,1)}) custom-call(bf16[32,4096]{1,0:T(8,128)(2,1)} %q_hbm.1, bf16[32,512]{1,0:T(8,128)(2,1)} %k_hbm.1, bf16[32,512]{1,0:T(8,128)(2,1)} %v_hbm.1, bf16[32,4096]{1,0:T(8,128)(2,1)} %o_hbm.1, bf16[32,4096]{1,0:T(8,128)(2,1)} %g_hbm.1, ...), custom_call_target="tpu_custom_call" | custom-call | tf_op jit(solution)/shard_map/pallas_call | solution.py:573
  70.2 0.0 copy-start.1
  70.2 1.7 %copy.13 = bf16[32,4096]{1,0:T(8,128)(2,1)} copy(bf16[32,4096]{1,0:T(8,128)(2,1)} %get-tuple-element.6) | data formatting | bytes 524288
  71.9 0.0 copy-done.1
  71.9 0.0 copy-start
  71.9 0.6 copy.14
  72.5 0.2 copy-done
  72.6 0.6 copy.15
Async XLA Ops:
  70.2 1.7 %copy-start.1 = (bf16[32,512]{1,0:T(8,128)(2,1)S(1)}, bf16[32,512]{1,0:T(8,128)(2,1)}, u32[]{:S(2)}) copy-start(bf16[32,512]{1,0:T(8,128)(2,1)} %get-tuple-element.7) | copy-start | bytes 98308
  71.9 0.8 %copy-start = (bf16[32,512]{1,0:T(8,128)(2,1)S(1)}, bf16[32,512]{1,0:T(8,128)(2,1)}, u32[]{:S(2)}) copy-start(bf16[32,512]{1,0:T(8,128)(2,1)} %get-tuple-element.8) | copy-start | bytes 98308

commit v3 on v2

--- a/solution.py
+++ b/solution.py
@@ -14,7 +14,6 @@
 SUB = TOK // 2
 PLANE = 32
 HALF = PLANE * SUB
-Q_ROWS = 2 * HALF
 PART = 256
 RUN = 128
 Z = 8
@@ -281,7 +280,7 @@
             run_of == r, pos_ref[z * 4 + r // 2, (r % 2) * RUN], run_start
         )
     for t in range(2):
-        qpos[0:1, t * HALF : (t + 1) * HALF] = run_start + inside + t * SUB
+        qpos[t, 0:1, :] = run_start + inside + t * SUB
     acc[...] = jnp.zeros_like(acc)
     dqt[...] = jnp.zeros_like(dqt)
 
@@ -289,8 +288,7 @@
     ones = jnp.ones((2 * PART, D), BF)
 
     def local_head(n):
-        own = core if n % 2 == 0 else 1 - core
-        return 2 * own + n // 2
+        return 2 * ((core + n) % 2) + n // 2
 
     def queries_of(n, t, r):
         first = r // SUB
@@ -302,49 +300,48 @@
 
     def prepare(n, t):
         for r in range(0, HALF, QT):
-            cols = slice(t * HALF + r, t * HALF + r + QT)
-            qt[n, 0:D, cols] = queries_of(n, t, r).T
-            gt[n, 0:D, cols] = cotangents_of(n, t, r).T
+            cols = slice(r, r + QT)
+            qt[n, t, 0:D, cols] = queries_of(n, t, r).T
+            gt[n, t, 0:D, cols] = cotangents_of(n, t, r).T
         first = 32 * t + 6 * local_head(n)
-        cols = slice(t * HALF, (t + 1) * HALF)
         every = auxt[...]
         empty = jnp.zeros_like(every)
-        qt[n, D : 2 * D, cols] = jnp.where(
+        qt[n, t, D : 2 * D, :] = jnp.where(
             (aux_row >= first) & (aux_row < first + 3), every, empty
         )
-        gt[n, D : 2 * D, cols] = jnp.where(
+        gt[n, t, D : 2 * D, :] = jnp.where(
             (aux_row >= first + 3) & (aux_row < first + 6), every, empty
         )
 
     key_iota = lax.broadcasted_iota(jnp.int32, (RUN, QT), 0)
 
-    def attend(heads, halves, a, c):
-        keys = jnp.concatenate([kv[a, 0], kv[c, 0]], axis=0)
-        values = jnp.concatenate([kv[a, 1], kv[c, 1]], axis=0)
+    def attend(heads, halves, slots):
+        keys = jnp.concatenate([kv[slot, 0] for slot in slots], axis=0)
+        values = jnp.concatenate([kv[slot, 1] for slot in slots], axis=0)
         keys_wide = jnp.concatenate([keys, ones], axis=1)
         values_wide = jnp.concatenate([values, ones], axis=1)
         keys_t = keys.T
         starts = []
-        for j in range(4):
-            slot = a if j < 2 else c
-            row = ((z + slot) % Z) * 4 + (j % 2) * 2 + core
-            starts.append(pos_ref[row, x_lo * RUN])
+        for slot in slots:
+            for half in range(2):
+                row = ((z + slot) % Z) * 4 + half * 2 + core
+                starts.append(pos_ref[row, x_lo * RUN])
         dk = jnp.zeros((2 * PART, D), F32)
         dv = jnp.zeros((2 * PART, D), F32)
         for n in heads:
             for t in halves:
                 for r in range(0, HALF, QT):
-                    cols = slice(t * HALF + r, t * HALF + r + QT)
-                    scores = jnp.dot(keys_wide, qt[n, :, cols], preferred_element_type=F32)
-                    shifted = jnp.dot(values_wide, gt[n, :, cols], preferred_element_type=F32)
+                    cols = slice(r, r + QT)
+                    scores = jnp.dot(keys_wide, qt[n, t, :, cols], preferred_element_type=F32)
+                    shifted = jnp.dot(values_wide, gt[n, t, :, cols], preferred_element_type=F32)
                     raw = jnp.exp2(scores * EXP2_SCALE)
-                    where = qpos[0:1, cols]
+                    where = qpos[t, 0:1, cols]
                     probs = jnp.concatenate(
                         [
                             jnp.where(
-                                where - starts[j] >= key_iota, raw[j * RUN : (j + 1) * RUN], 0.0
+                                where - start >= key_iota, raw[m * RUN : (m + 1) * RUN], 0.0
                             )
-                            for j in range(4)
+                            for m, start in enumerate(starts)
                         ],
                         axis=0,
                     )
@@ -355,16 +352,13 @@
                     dk = dk + jnp.dot(
                         score_grad, queries_of(n, t, r), preferred_element_type=F32
                     )
-                    dqt[n, :, cols] += jnp.dot(
+                    dqt[n, t, :, cols] += jnp.dot(
                         keys_t, score_grad, preferred_element_type=F32
                     )
-        acc[a, 0] += dk[:PART]
-        acc[c, 0] += dk[PART:]
-        acc[a, 1] += dv[:PART]
-        acc[c, 1] += dv[PART:]
-
-    def slots_of(i):
-        return 7 - i, (1 + i) % 4
+        for m, slot in enumerate(slots):
+            rows = slice(m * PART, (m + 1) * PART)
+            acc[slot, 0] += dk[rows]
+            acc[slot, 1] += dv[rows]
 
     def swap(k):
         return pltpu.make_async_remote_copy(
@@ -377,8 +371,11 @@
         )
 
     def swap_start(k):
-        for r in range(0, Q_ROWS, QT):
-            dqx_send[k, r : r + QT, :] = (dqt[2 * k + 1, :, r : r + QT] * SCALE).T.astype(BF)
+        for t in range(2):
+            for r in range(0, HALF, QT):
+                dqx_send[k, t, r : r + QT, :] = (
+                    (dqt[2 * k + 1, t, :, r : r + QT] * SCALE).T.astype(BF)
+                )
         swap(k).start()
 
     def dq_columns(k):
@@ -398,12 +395,14 @@
 
     def send_dq(k):
         swap(k).wait_recv()
-        for r in range(0, Q_ROWS, QT):
-            total = (dqt[2 * k, :, r : r + QT] * SCALE).T + dqx[k, r : r + QT, :].astype(F32)
-            first = (r % HALF) // SUB
-            dqs[k, r // HALF, first : first + QT // SUB] = total.astype(BF).reshape(
-                QT // SUB, SUB, D
-            )
+        for t in range(2):
+            for r in range(0, HALF, QT):
+                total = (dqt[2 * k, t, :, r : r + QT] * SCALE).T
+                total = total + dqx[k, t, r : r + QT, :].astype(F32)
+                first = r // SUB
+                dqs[k, t, first : first + QT // SUB] = total.astype(BF).reshape(
+                    QT // SUB, SUB, D
+                )
 
         def body(i, carry):
             dq_copy(k, i).start()
@@ -426,108 +425,143 @@
             device_id_type=MESH,
         )
 
+    def rs_copy(src, dst, which, device):
+        return pltpu.make_async_remote_copy(
+            src_ref=rs_send.at[src, which],
+            dst_ref=rs.at[dst, which],
+            send_sem=rs_send_sem.at[which, dst],
+            recv_sem=rs_recv_sem.at[which, dst],
+            device_id=device,
+            device_id_type=MESH,
+        )
+
+    def reduce_step(slot, first):
+        onward, device = (slot - 1, right) if slot < 4 else (slot + 1, left)
+        for which in range(2):
+            if not first:
+                rs_copy(0, slot, which, right).wait_recv()
+                acc[slot, which] += rs[slot, which].astype(F32)
+            rs_send[slot, which] = acc[slot, which].astype(BF)
+            if slot in (1, 7):
+                out_start(slot, which)
+            else:
+                rs_copy(slot, onward, which, device).start()
+
+    out_kinds = {0: 0, 1: 1, 7: 2, 4: 3}
+
+    def out_copy(slot, i, which):
+        j = (my_j + i) % 8
+        rows = pl.ds(pl.multiple_of((j // 4) * RUN + (j % 4) * TOK, TOK), TOK)
+        kind = out_kinds[slot]
+        plane = (z + slot) % Z
+        return pltpu.make_async_remote_copy(
+            src_ref=rs_send.at[slot, which, rows, :],
+            dst_ref=kv_recv.at[kind, x_hi, which, :, own_cols],
+            send_sem=out_send_sem.at[kind, which, i],
+            recv_sem=out_recv_sem,
+            device_id=(x_lo * 4 + j % 4, plane * 4 + (j // 4) * 2 + core),
+            device_id_type=MESH,
+        )
+
+    def out_start(slot, which):
+        def body(i, carry):
+            out_copy(slot, i, which).start()
+            return carry
+
+        lax.fori_loop(1 if slot == 0 else 0, 8, body, 0)
+        if slot == 0:
+            pltpu.make_async_copy(
+                rs_send.at[0, which, key_rows, :],
+                kv_recv.at[0, x_hi, which, :, own_cols],
+                out_recv_sem,
+            ).start()
+
+    def out_direct(slot):
+        for which in range(2):
+            rs_send[slot, which] = acc[slot, which].astype(BF)
+            out_start(slot, which)
+
     all_of(qd.at[0, 0], q_recv_sem.at[0])
     forward(0).start()
     all_of(aux, q_recv_sem.at[3])
     auxt[...] = aux[...].reshape(HALF, D).T
     prepare(0, 0)
+
     ring_step(0)
     forward(0).wait_recv()
     prepare(1, 0)
-    attend((0, 1), (0,), 7, 1)
+    attend((0, 1), (0,), (7, 1))
     all_of(qd.at[0, 1], q_recv_sem.at[1])
     forward(1).start()
     prepare(0, 1)
     forward(1).wait_recv()
     prepare(1, 1)
-    attend((0, 1), (1,), 7, 1)
-
-    def first_heads(i, carry):
-        ring_step(i)
-        a, c = slots_of(i)
-        attend((0, 1), (0, 1), a, c)
+    attend((0, 1), (1,), (7, 1))
+
+    steps = ((1, 0), (2, 0), (2, 1), (1, 1), (3, 0), (3, 1))
+
+    def step_of(s, carry):
+        pair, head = carry[0] % 4, 2 * (carry[1] % 2)
+
+        @pl.when(s == 0)
+        def _():
+            ring_step(1)
+
+        @pl.when(s == 1)
+        def _():
+            ring_step(2)
+            all_of(qd.at[2], q_recv_sem.at[2])
+            forward(2).start()
+
+        @pl.when(s == 2)
+        def _():
+            prepare(2, 0)
+            prepare(2, 1)
+            forward(2).wait_recv()
+            prepare(3, 0)
+            prepare(3, 1)
+
+        @pl.when(s == 3)
+        def _():
+            reduce_step(5, True)
+            reduce_step(3, True)
+            ring_step(3)
+
+        @pl.when(s == 5)
+        def _():
+            reduce_step(6, False)
+            reduce_step(2, False)
+            swap_start(0)
+
+        attend((head, head + 1), (0, 1), (7 - pair, (1 + pair) % 4))
+        return carry[0] // 4, carry[1] // 2
+
+    lax.fori_loop(
+        0,
+        len(steps),
+        step_of,
+        (
+            jnp.int32(sum(pair * 4**s for s, (pair, _) in enumerate(steps))),
+            jnp.int32(sum(head * 2**s for s, (_, head) in enumerate(steps))),
+        ),
+    )
+    out_direct(4)
+    out_direct(0)
+    send_dq(0)
+
+    def last(u, carry):
+        attend((3 - u,), (0, 1), (7, 1))
+
+        @pl.when(u == 0)
+        def _():
+            swap_start(1)
+
         return carry
 
-    lax.fori_loop(1, 4, first_heads, 0)
-    swap_start(0)
-
-    all_of(qd.at[2], q_recv_sem.at[2])
-    forward(2).start()
-    prepare(2, 0)
-    prepare(2, 1)
-    send_dq(0)
-    forward(2).wait_recv()
-    prepare(3, 0)
-    prepare(3, 1)
-
-    def rs_copy(src, dst, which, device):
-        return pltpu.make_async_remote_copy(
-            src_ref=rs_send.at[src, which],
-            dst_ref=rs.at[dst, which],
-            send_sem=rs_send_sem.at[which, dst],
-            recv_sem=rs_recv_sem.at[which, dst],
-            device_id=device,
-            device_id_type=MESH,
-        )
-
-    def last_heads(step, carry):
-        a, c = slots_of(3 - step)
-        attend((2, 3), (0, 1), a, c)
-        down = 4 - step
-        up = 4 + step
-        for which in range(2):
-
-            @pl.when(step > 0)
-            def _(which=which):
-                rs_copy(0, down, which, right).wait_recv()
-                acc[down, which] += rs[down, which].astype(F32)
-
-            rs_send[down, which] = acc[down, which].astype(BF)
-            rs_copy(down, down - 1, which, right).start()
-
-            @pl.when(step > 1)
-            def _(which=which):
-                rs_copy(0, up, which, left).wait_recv()
-                acc[up, which] += rs[up, which].astype(F32)
-
-            @pl.when(step > 0)
-            def _(which=which):
-                rs_send[up, which] = acc[up, which].astype(BF)
-                rs_copy(up, up + 1 - 4 * (up // 7), which, left).start()
-
-        return carry
-
-    lax.fori_loop(0, 4, last_heads, 0)
-    swap_start(1)
+    lax.fori_loop(0, 2, last, 0)
+    reduce_step(1, False)
+    reduce_step(7, False)
     send_dq(1)
-
-    def out_copy(i, which):
-        j = (my_j + i) % 8
-        rows = pl.ds(pl.multiple_of((j // 4) * RUN + (j % 4) * TOK, TOK), TOK)
-        return pltpu.make_async_remote_copy(
-            src_ref=rs_send.at[0, which, rows, :],
-            dst_ref=kv_recv.at[x_hi, which, :, own_cols],
-            send_sem=out_send_sem.at[which, i],
-            recv_sem=out_recv_sem,
-            device_id=part_device(j),
-            device_id_type=MESH,
-        )
-
-    for which in range(2):
-        rs_copy(0, 4, which, left).wait_recv()
-        rs_copy(0, 0, which, right).wait_recv()
-        rs_send[0, which] = (
-            acc[0, which] + rs[4, which].astype(F32) + rs[0, which].astype(F32)
-        ).astype(BF)
-
-        def out_start(i, carry, which=which):
-            out_copy(i, which).start()
-            return carry
-
-        lax.fori_loop(1, 8, out_start, 0)
-        pltpu.make_async_copy(
-            rs_send.at[0, which, key_rows, :], kv_recv.at[x_hi, which, :, own_cols], out_recv_sem
-        ).start()
 
     all_of(dq_recv, dq_recv_sem)
     for t in range(2):
@@ -536,8 +570,15 @@
             total = dq_recv[0, t, :, cols].astype(F32) + dq_recv[1, t, :, cols].astype(F32)
             dq_out[t * SUB : (t + 1) * SUB, cols] = total.astype(BF)
     all_of(kv_recv, out_recv_sem)
-    dk_out[...] = ((kv_recv[0, 0].astype(F32) + kv_recv[1, 0].astype(F32)) * SCALE).astype(BF)
-    dv_out[...] = (kv_recv[0, 1].astype(F32) + kv_recv[1, 1].astype(F32)).astype(BF)
+    sums = []
+    for which in range(2):
+        total = jnp.zeros((TOK, KVH * D), F32)
+        for kind in range(4):
+            for hh in range(2):
+                total = total + kv_recv[kind, hh, which].astype(F32)
+        sums.append(total)
+    dk_out[...] = (sums[0] * SCALE).astype(BF)
+    dv_out[...] = sums[1].astype(BF)
 
     def finish_plane(i, carry):
         for stage in range(4):
@@ -551,7 +592,8 @@
     def finish_part(i, carry):
         for which in range(2):
             kv_copy(i, which).wait_send()
-            out_copy(i, which).wait_send()
+            for slot in (0, 1, 7, 4):
+                out_copy(slot, i, which).wait_send()
         return carry
 
     lax.fori_loop(1, 8, finish_part, 0)
@@ -560,9 +602,11 @@
     for k in range(2):
         swap(k).wait_send()
     for which in range(2):
+        for slot in (1, 7, 4):
+            out_copy(slot, 0, which).wait_send()
         for dst in range(1, 8):
             ring_copy(0, dst, which, right).wait_send()
-        for dst in (0, 1, 2, 3, 4, 6, 7):
+        for dst in (1, 2, 6, 7):
             rs_copy(0, dst, which, right).wait_send()
 
 
@@ -592,19 +636,19 @@
             pltpu.VMEM((LOCAL, 2, PLANE, 2 * SUB, D), BF),
             pltpu.VMEM((PLANE, SUB, D), BF),
             pltpu.VMEM((D, HALF), BF),
-            pltpu.VMEM((LOCAL, 2 * D, Q_ROWS), BF),
-            pltpu.VMEM((LOCAL, 2 * D, Q_ROWS), BF),
-            pltpu.VMEM((8, Q_ROWS), jnp.int32),
+            pltpu.VMEM((LOCAL, 2, 2 * D, HALF), BF),
+            pltpu.VMEM((LOCAL, 2, 2 * D, HALF), BF),
+            pltpu.VMEM((2, 8, HALF), jnp.int32),
             pltpu.VMEM((Z, 2, PART, D), BF),
             pltpu.VMEM((Z, 2, PART, D), F32),
-            pltpu.VMEM((LOCAL, D, Q_ROWS), F32),
+            pltpu.VMEM((LOCAL, 2, D, HALF), F32),
             pltpu.VMEM((2, 2, PLANE, SUB, D), BF),
-            pltpu.VMEM((2, Q_ROWS, D), BF),
-            pltpu.VMEM((2, Q_ROWS, D), BF),
+            pltpu.VMEM((2, 2, HALF, D), BF),
+            pltpu.VMEM((2, 2, HALF, D), BF),
             pltpu.VMEM((Z, 2, PART, D), BF),
             pltpu.VMEM((Z, 2, PART, D), BF),
             pltpu.VMEM((2, 2, SUB, HQ * D), BF),
-            pltpu.VMEM((2, 2, TOK, KVH * D), BF),
+            pltpu.VMEM((4, 2, 2, TOK, KVH * D), BF),
             dma((7,)),
             dma((4, PLANE)),
             dma((4,)),
@@ -620,7 +664,7 @@
             dma((2,)),
             dma((2, PLANE)),
             dma,
-            dma((2, 8)),
+            dma((4, 2, 8)),
             dma,
         ],
         compiler_params=pltpu.CompilerParams(

time: 73.4 us -> 70.7 us (0.963)
  Pallas kernels: 69.5 us -> 66.8 us
    pallas_call x1, Pallas kernels: 69.5 us -> 66.8 us  [shards(): pl.pallas_call(kernel, out_shape=(jax.ShapeDtypeStruct((TOK, HQ * D), BF)...]
where the time goes in v3:
time: 70.7 us; the launch traced here: 70.5 us
  Pallas kernels  66.8 us (94%)
  local copies, waits for them, and re-layouts  3.06 us (4%)
    pallas_call x1, Pallas kernels, shards(): pl.pallas_call(kernel, out_shape=(jax.ShapeDtypeStruct((TOK, HQ * D), BF)...  66.8 us
    unnamed x7, local copies, waits for them, and re-layouts  3.06 us

profile of v3, /device:TPU:1, one launch (start us, length us, event | category | flops | bytes accessed | tf_op | source)
XLA Modules:
  0.0 70.5 jit_solution(3127996749521402624)
XLA Ops:
  0.6 66.8 %shard_map.94 = (bf16[32,4096]{1,0:T(8,128)(2,1)}, bf16[32,512]{1,0:T(8,128)(2,1)}, bf16[32,512]{1,0:T(8,128)(2,1)}) custom-call(bf16[32,4096]{1,0:T(8,128)(2,1)} %q_hbm.1, bf16[32,512]{1,0:T(8,128)(2,1)} %k_hbm.1, bf16[32,512]{1,0:T(8,128)(2,1)} %v_hbm.1, bf16[32,4096]{1,0:T(8,128)(2,1)} %o_hbm.1, bf16[32,4096]{1,0:T(8,128)(2,1)} %g_hbm.1, ...), custom_call_target="tpu_custom_call" | custom-call | tf_op jit(solution)/shard_map/pallas_call | solution.py:617
  67.4 0.0 copy-start.1
  67.4 1.7 %copy.13 = bf16[32,4096]{1,0:T(8,128)(2,1)} copy(bf16[32,4096]{1,0:T(8,128)(2,1)} %get-tuple-element.6) | data formatting | bytes 524288
  69.1 0.0 copy-done.1
  69.1 0.0 copy-start
  69.1 0.6 copy.14
  69.7 0.2 copy-done
  69.9 0.6 copy.15
Async XLA Ops:
  67.4 1.7 %copy-start.1 = (bf16[32,512]{1,0:T(8,128)(2,1)S(1)}, bf16[32,512]{1,0:T(8,128)(2,1)}, u32[]{:S(2)}) copy-start(bf16[32,512]{1,0:T(8,128)(2,1)} %get-tuple-element.7) | copy-start | bytes 98308
  69.1 0.8 %copy-start = (bf16[32,512]{1,0:T(8,128)(2,1)S(1)}, bf16[32,512]{1,0:T(8,128)(2,1)}, u32[]{:S(2)}) copy-start(bf16[32,512]{1,0:T(8,128)(2,1)} %get-tuple-element.8) | copy-start | bytes 98308

commit v4 on v3

--- a/solution.py
+++ b/solution.py
@@ -53,9 +53,8 @@
     lse_ref,
     pos_ref,
     pack,
-    pack_aux,
+    pack_kv,
     qd,
-    aux,
     auxt,
     qt,
     gt,
@@ -155,22 +154,26 @@
                 part[t * SUB : (t + 1) * SUB], place, preferred_element_type=F32
             )
     aux_low = aux_sum.astype(BF)
-    for group in range(groups):
-        pack_aux[group] = aux_low[:, group * D : (group + 1) * D]
     for load in loads[3:]:
         load.wait()
     for hh in range(2):
         for c in range(2):
             for g in range(4):
+                slot = (hh * 2 + c) * 4 + g
+                group = g * 2 + hh
+                pack[slot, 0, 0, 2 * SUB : 3 * SUB, :] = aux_low[:, group * D : (group + 1) * D]
                 for j in range(2):
                     head = g * 8 + hh * 4 + 2 * c + j
                     cols = slice(head * D, (head + 1) * D)
-                    slot = (hh * 2 + c) * 4 + g
                     for t in range(2):
                         rows = slice(t * SUB, (t + 1) * SUB)
                         pack[slot, j, t, 0:SUB, :] = q_ref[rows, cols]
                         pack[slot, j, t, SUB : 2 * SUB, :] = g_ref[rows, cols]
 
+    for g in range(KVH):
+        pack_kv[g, 0] = k_ref[:, g * D : (g + 1) * D]
+        pack_kv[g, 1] = v_ref[:, g * D : (g + 1) * D]
+
     pl.semaphore_wait(barrier, PLANE + 1)
 
     key_rows = pl.ds(pl.multiple_of(x_hi * RUN + y * TOK, TOK), TOK)
@@ -179,40 +182,34 @@
     def part_device(j):
         return (x_lo * 4 + j % 4, z * 4 + (j // 4) * 2 + core)
 
-    def kv_copy(i, which):
+    def kv_copy(i):
         j = (my_j + i) % 8
-        src = (k_ref, v_ref)[which]
-        cols = pl.ds(pl.multiple_of((j % 4) * D, D), D)
-        return pltpu.make_async_remote_copy(
-            src_ref=src.at[:, cols],
-            dst_ref=kv.at[0, which, key_rows, :],
-            send_sem=kv_send_sem.at[which, i],
-            recv_sem=kv_recv_sem.at[which],
+        return pltpu.make_async_remote_copy(
+            src_ref=pack_kv.at[j % 4],
+            dst_ref=kv.at[0, :, key_rows, :],
+            send_sem=kv_send_sem,
+            recv_sem=kv_recv_sem,
             device_id=part_device(j),
             device_id_type=MESH,
         )
 
     own_cols = pl.ds(pl.multiple_of(y * D, D), D)
-    for which in range(2):
-
-        def kv_start(i, carry, which=which):
-            kv_copy(i, which).start()
-            return carry
-
-        lax.fori_loop(1, 8, kv_start, 0)
-        pltpu.make_async_copy(
-            (k_ref, v_ref)[which].at[:, own_cols],
-            kv.at[0, which, key_rows, :],
-            kv_recv_sem.at[which],
-        ).start()
+
+    def kv_start(i, carry):
+        kv_copy(i).start()
+        return carry
+
+    lax.fori_loop(1, 8, kv_start, 0)
+    pltpu.make_async_copy(pack_kv.at[y], kv.at[0, :, key_rows, :], kv_recv_sem).start()
 
     def q_ends(stage, p):
         slot = (p // 8) * 4 + p % 4
-        if stage < 2:
-            return pack.at[slot, 0, stage], qd.at[0, stage, me]
-        if stage == 2:
-            return pack.at[slot, 1], qd.at[2, :, me]
-        return pack_aux.at[(p % 4) * 2 + p // 16], aux.at[me]
+        if stage == 0:
+            return pack.at[slot, 0, 0], qd.at[0, 0, me]
+        rows = slice(0, 2 * SUB)
+        if stage == 1:
+            return pack.at[slot, 0, 1, rows], qd.at[0, 1, me, rows]
+        return pack.at[slot, 1, :, rows], qd.at[2, :, me, rows]
 
     def q_copy(stage, i):
         p = (me + i) % PLANE
@@ -220,22 +217,20 @@
         return pltpu.make_async_remote_copy(
             src_ref=src,
             dst_ref=dst,
-            send_sem=q_send_sem.at[stage, i],
+            send_sem=q_send_sem.at[stage],
             recv_sem=q_recv_sem.at[stage],
             device_id=plane_device(p),
             device_id_type=MESH,
         )
 
-    def q_start(stages):
+    def q_start(stage):
         def body(i, carry):
-            for stage in stages:
-                q_copy(stage, i).start()
+            q_copy(stage, i).start()
             return carry
 
         lax.fori_loop(1, PLANE, body, 0)
-        for stage in stages:
-            src, dst = q_ends(stage, me)
-            pltpu.make_async_copy(src, dst, q_recv_sem.at[stage]).start()
+        src, dst = q_ends(stage, me)
+        pltpu.make_async_copy(src, dst, q_recv_sem.at[stage]).start()
 
     def all_of(ref, sem):
         pltpu.make_async_copy(ref, ref, sem).wait()
@@ -263,13 +258,13 @@
             def _(which=which):
                 ring_copy(1 + i, 2 + i, which, left).start()
 
-    q_start((0, 3))
+    q_start(0)
+    q_start(1)
+    all_of(kv.at[0], kv_recv_sem)
     for which in range(2):
-        all_of(kv.at[0, which], kv_recv_sem.at[which])
         ring_copy(0, 7, which, right).start()
         ring_copy(0, 1, which, left).start()
-    q_start((1,))
-    q_start((2,))
+    q_start(2)
 
     lane = lax.broadcasted_iota(jnp.int32, (1, HALF), 1)
     run_of = lax.shift_right_logical(lane, 6)
@@ -387,7 +382,7 @@
         return pltpu.make_async_remote_copy(
             src_ref=dqs.at[k, :, p],
             dst_ref=dq_recv.at[x_lo, :, :, dq_columns(k)],
-            send_sem=dq_send_sem.at[k, i],
+            send_sem=dq_send_sem.at[k],
             recv_sem=dq_recv_sem,
             device_id=plane_device(p),
             device_id_type=MESH,
@@ -414,8 +409,9 @@
         ).start()
 
     def forward(stage):
-        src = qd.at[0, stage] if stage < 2 else qd.at[2]
-        dst = qd.at[1, stage] if stage < 2 else qd.at[3]
+        rows = slice(0, 2 * SUB)
+        src = qd.at[0, stage, :, rows] if stage < 2 else qd.at[2, :, :, rows]
+        dst = qd.at[1, stage, :, rows] if stage < 2 else qd.at[3, :, :, rows]
         return pltpu.make_async_remote_copy(
             src_ref=src,
             dst_ref=dst,
@@ -442,57 +438,57 @@
                 rs_copy(0, slot, which, right).wait_recv()
                 acc[slot, which] += rs[slot, which].astype(F32)
             rs_send[slot, which] = acc[slot, which].astype(BF)
-            if slot in (1, 7):
-                out_start(slot, which)
-            else:
+            if slot not in (1, 7):
                 rs_copy(slot, onward, which, device).start()
+        if slot in (1, 7):
+            out_start(slot)
 
     out_kinds = {0: 0, 1: 1, 7: 2, 4: 3}
 
-    def out_copy(slot, i, which):
+    def out_copy(slot, i):
         j = (my_j + i) % 8
         rows = pl.ds(pl.multiple_of((j // 4) * RUN + (j % 4) * TOK, TOK), TOK)
         kind = out_kinds[slot]
         plane = (z + slot) % Z
         return pltpu.make_async_remote_copy(
-            src_ref=rs_send.at[slot, which, rows, :],
-            dst_ref=kv_recv.at[kind, x_hi, which, :, own_cols],
-            send_sem=out_send_sem.at[kind, which, i],
+            src_ref=rs_send.at[slot, :, rows, :],
+            dst_ref=kv_recv.at[kind, x_hi, :, :, own_cols],
+            send_sem=out_send_sem.at[kind],
             recv_sem=out_recv_sem,
             device_id=(x_lo * 4 + j % 4, plane * 4 + (j // 4) * 2 + core),
             device_id_type=MESH,
         )
 
-    def out_start(slot, which):
+    def out_start(slot):
         def body(i, carry):
-            out_copy(slot, i, which).start()
+            out_copy(slot, i).start()
             return carry
 
         lax.fori_loop(1 if slot == 0 else 0, 8, body, 0)
         if slot == 0:
             pltpu.make_async_copy(
-                rs_send.at[0, which, key_rows, :],
-                kv_recv.at[0, x_hi, which, :, own_cols],
+                rs_send.at[0, :, key_rows, :],
+                kv_recv.at[0, x_hi, :, :, own_cols],
                 out_recv_sem,
             ).start()
 
     def out_direct(slot):
-        for which in range(2):
-            rs_send[slot, which] = acc[slot, which].astype(BF)
-            out_start(slot, which)
+        rs_send[slot] = acc[slot].astype(BF)
+        out_start(slot)
 
     all_of(qd.at[0, 0], q_recv_sem.at[0])
     forward(0).start()
-    all_of(aux, q_recv_sem.at[3])
-    auxt[...] = aux[...].reshape(HALF, D).T
+    auxt[...] = qd[0, 0, :, 2 * SUB : 3 * SUB, :].reshape(HALF, D).T
     prepare(0, 0)
 
     ring_step(0)
     forward(0).wait_recv()
     prepare(1, 0)
+    second_half = qd.at[0, 1, :, 0 : 2 * SUB]
+    all_of(second_half, q_recv_sem.at[1])
+    forward(1).start()
     attend((0, 1), (0,), (7, 1))
-    all_of(qd.at[0, 1], q_recv_sem.at[1])
-    forward(1).start()
+    ring_step(1)
     prepare(0, 1)
     forward(1).wait_recv()
     prepare(1, 1)
@@ -503,14 +499,10 @@
     def step_of(s, carry):
         pair, head = carry[0] % 4, 2 * (carry[1] % 2)
 
-        @pl.when(s == 0)
-        def _():
-            ring_step(1)
-
         @pl.when(s == 1)
         def _():
             ring_step(2)
-            all_of(qd.at[2], q_recv_sem.at[2])
+            all_of(qd.at[2, :, :, 0 : 2 * SUB], q_recv_sem.at[2])
             forward(2).start()
 
         @pl.when(s == 2)
@@ -580,30 +572,20 @@
     dk_out[...] = (sums[0] * SCALE).astype(BF)
     dv_out[...] = sums[1].astype(BF)
 
-    def finish_plane(i, carry):
-        for stage in range(4):
-            q_copy(stage, i).wait_send()
-        for k in range(2):
-            dq_copy(k, i).wait_send()
-        return carry
-
-    lax.fori_loop(1, PLANE, finish_plane, 0)
-
-    def finish_part(i, carry):
-        for which in range(2):
-            kv_copy(i, which).wait_send()
-            for slot in (0, 1, 7, 4):
-                out_copy(slot, i, which).wait_send()
-        return carry
-
-    lax.fori_loop(1, 8, finish_part, 0)
+    others = PLANE - 1
+    all_of(qd.at[0, 0, 0:others], q_send_sem.at[0])
+    all_of(qd.at[0, 1, 0:others, 0 : 2 * SUB], q_send_sem.at[1])
+    all_of(qd.at[2, :, 0:others, 0 : 2 * SUB], q_send_sem.at[2])
+    all_of(kv.at[0, :, 0 : 7 * TOK], kv_send_sem)
+    for k in range(2):
+        all_of(dqs.at[k, :, 0:others], dq_send_sem.at[k])
+        swap(k).wait_send()
+    for slot in (1, 7, 4):
+        all_of(rs_send.at[slot], out_send_sem.at[out_kinds[slot]])
+    all_of(rs_send.at[0, :, 0 : 7 * TOK], out_send_sem.at[0])
     for stage in range(3):
         forward(stage).wait_send()
-    for k in range(2):
-        swap(k).wait_send()
     for which in range(2):
-        for slot in (1, 7, 4):
-            out_copy(slot, 0, which).wait_send()
         for dst in range(1, 8):
             ring_copy(0, dst, which, right).wait_send()
         for dst in (1, 2, 6, 7):
@@ -631,10 +613,9 @@
             pltpu.VMEM((TOK, HQ * D), BF),
             pltpu.VMEM((TOK, HQ), BF),
             pltpu.SMEM((32, 256), jnp.int32),
-            pltpu.VMEM((16, 2, 2, 2 * SUB, D), BF),
-            pltpu.VMEM((8, SUB, D), BF),
-            pltpu.VMEM((LOCAL, 2, PLANE, 2 * SUB, D), BF),
-            pltpu.VMEM((PLANE, SUB, D), BF),
+            pltpu.VMEM((16, 2, 2, 3 * SUB, D), BF),
+            pltpu.VMEM((KVH, 2, TOK, D), BF),
+            pltpu.VMEM((LOCAL, 2, PLANE, 3 * SUB, D), BF),
             pltpu.VMEM((D, HALF), BF),
             pltpu.VMEM((LOCAL, 2, 2 * D, HALF), BF),
             pltpu.VMEM((LOCAL, 2, 2 * D, HALF), BF),
@@ -650,21 +631,21 @@
             pltpu.VMEM((2, 2, SUB, HQ * D), BF),
             pltpu.VMEM((4, 2, 2, TOK, KVH * D), BF),
             dma((7,)),
-            dma((4, PLANE)),
-            dma((4,)),
             dma((3,)),
             dma((3,)),
-            dma((2, 8)),
-            dma((2,)),
+            dma((3,)),
+            dma((3,)),
+            dma,
+            dma,
             dma((2, Z)),
             dma((2, Z)),
             dma((2, Z)),
             dma((2, Z)),
             dma((2,)),
             dma((2,)),
-            dma((2, PLANE)),
+            dma((2,)),
             dma,
-            dma((4, 2, 8)),
+            dma((4,)),
             dma,
         ],
         compiler_params=pltpu.CompilerParams(

time: 70.7 us -> 66.9 us (0.946)
  Pallas kernels: 66.8 us -> 63 us
    pallas_call x1, Pallas kernels: 66.8 us -> 63 us  [shards(): pl.pallas_call(kernel, out_shape=(jax.ShapeDtypeStruct((TOK, HQ * D), BF)...]
where the time goes in v4:
time: 66.9 us; the launch traced here: 66.7 us
  Pallas kernels  63 us (94%)
  local copies, waits for them, and re-layouts  3.06 us (5%)
    pallas_call x1, Pallas kernels, shards(): pl.pallas_call(kernel, out_shape=(jax.ShapeDtypeStruct((TOK, HQ * D), BF)...  63 us
    unnamed x7, local copies, waits for them, and re-layouts  3.06 us

profile of v4, /device:TPU:1, one launch (start us, length us, event | category | flops | bytes accessed | tf_op | source)
XLA Modules:
  0.0 66.7 jit_solution(2177580558176738434)
XLA Ops:
  0.6 63.0 %shard_map.94 = (bf16[32,4096]{1,0:T(8,128)(2,1)}, bf16[32,512]{1,0:T(8,128)(2,1)}, bf16[32,512]{1,0:T(8,128)(2,1)}) custom-call(bf16[32,4096]{1,0:T(8,128)(2,1)} %q_hbm.1, bf16[32,512]{1,0:T(8,128)(2,1)} %k_hbm.1, bf16[32,512]{1,0:T(8,128)(2,1)} %v_hbm.1, bf16[32,4096]{1,0:T(8,128)(2,1)} %o_hbm.1, bf16[32,4096]{1,0:T(8,128)(2,1)} %g_hbm.1, ...), custom_call_target="tpu_custom_call" | custom-call | tf_op jit(solution)/shard_map/pallas_call | solution.py:599
  63.6 0.0 copy-start.1
  63.7 1.7 %copy.13 = bf16[32,4096]{1,0:T(8,128)(2,1)} copy(bf16[32,4096]{1,0:T(8,128)(2,1)} %get-tuple-element.6) | data formatting | bytes 524288
  65.3 0.0 copy-done.1
  65.3 0.0 copy-start
  65.3 0.6 copy.14
  66.0 0.2 copy-done
  66.1 0.6 copy.15
Async XLA Ops:
  63.6 1.7 %copy-start.1 = (bf16[32,512]{1,0:T(8,128)(2,1)S(1)}, bf16[32,512]{1,0:T(8,128)(2,1)}, u32[]{:S(2)}) copy-start(bf16[32,512]{1,0:T(8,128)(2,1)} %get-tuple-element.7) | copy-start | bytes 98308
  65.3 0.8 %copy-start = (bf16[32,512]{1,0:T(8,128)(2,1)S(1)}, bf16[32,512]{1,0:T(8,128)(2,1)}, u32[]{:S(2)}) copy-start(bf16[32,512]{1,0:T(8,128)(2,1)} %get-tuple-element.8) | copy-start | bytes 98308

commit v5 on v4

--- a/solution.py
+++ b/solution.py
@@ -42,9 +42,8 @@
     g_hbm,
     lse_hbm,
     pos_hbm,
-    dq_out,
-    dk_out,
-    dv_out,
+    dq_recv,
+    kv_recv,
     q_ref,
     k_ref,
     v_ref,
@@ -67,8 +66,6 @@
     dqx,
     rs_send,
     rs,
-    dq_recv,
-    kv_recv,
     in_sem,
     q_send_sem,
     q_recv_sem,
@@ -476,36 +473,52 @@
         rs_send[slot] = acc[slot].astype(BF)
         out_start(slot)
 
+    ring_step(0)
     all_of(qd.at[0, 0], q_recv_sem.at[0])
     forward(0).start()
     auxt[...] = qd[0, 0, :, 2 * SUB : 3 * SUB, :].reshape(HALF, D).T
     prepare(0, 0)
 
-    ring_step(0)
-    forward(0).wait_recv()
-    prepare(1, 0)
-    second_half = qd.at[0, 1, :, 0 : 2 * SUB]
-    all_of(second_half, q_recv_sem.at[1])
+    def nearest(n, carry):
+        @pl.when(n == 1)
+        def _():
+            forward(0).wait_recv()
+            prepare(1, 0)
+
+        attend((n,), (0,), (7, 1))
+        return carry
+
+    lax.fori_loop(0, 2, nearest, 0)
+    ring_step(1)
+    all_of(qd.at[0, 1, :, 0 : 2 * SUB], q_recv_sem.at[1])
     forward(1).start()
-    attend((0, 1), (0,), (7, 1))
-    ring_step(1)
-    prepare(0, 1)
-    forward(1).wait_recv()
-    prepare(1, 1)
-    attend((0, 1), (1,), (7, 1))
-
-    steps = ((1, 0), (2, 0), (2, 1), (1, 1), (3, 0), (3, 1))
+
+    def halves(u, carry):
+        t, pair = (u + 1) // 2, (u + 1) % 2
+
+        @pl.when(u == 1)
+        def _():
+            prepare(0, 1)
+            forward(1).wait_recv()
+            prepare(1, 1)
+
+        attend((0, 1), (t,), (7 - pair, 1 + pair))
+        return carry
+
+    lax.fori_loop(0, 3, halves, 0)
+
+    steps = ((2, 0), (2, 1), (1, 1), (3, 0), (3, 1))
 
     def step_of(s, carry):
         pair, head = carry[0] % 4, 2 * (carry[1] % 2)
 
-        @pl.when(s == 1)
+        @pl.when(s == 0)
         def _():
             ring_step(2)
             all_of(qd.at[2, :, :, 0 : 2 * SUB], q_recv_sem.at[2])
             forward(2).start()
 
-        @pl.when(s == 2)
+        @pl.when(s == 1)
         def _():
             prepare(2, 0)
             prepare(2, 1)
@@ -513,13 +526,16 @@
             prepare(3, 0)
             prepare(3, 1)
 
-        @pl.when(s == 3)
+        @pl.when(s == 2)
         def _():
             reduce_step(5, True)
             reduce_step(3, True)
+
+        @pl.when(s == 3)
+        def _():
             ring_step(3)
 
-        @pl.when(s == 5)
+        @pl.when(s == 4)
         def _():
             reduce_step(6, False)
             reduce_step(2, False)
@@ -556,21 +572,7 @@
     send_dq(1)
 
     all_of(dq_recv, dq_recv_sem)
-    for t in range(2):
-        for r in range(0, HQ * D, 512):
-            cols = slice(r, r + 512)
-            total = dq_recv[0, t, :, cols].astype(F32) + dq_recv[1, t, :, cols].astype(F32)
-            dq_out[t * SUB : (t + 1) * SUB, cols] = total.astype(BF)
     all_of(kv_recv, out_recv_sem)
-    sums = []
-    for which in range(2):
-        total = jnp.zeros((TOK, KVH * D), F32)
-        for kind in range(4):
-            for hh in range(2):
-                total = total + kv_recv[kind, hh, which].astype(F32)
-        sums.append(total)
-    dk_out[...] = (sums[0] * SCALE).astype(BF)
-    dv_out[...] = sums[1].astype(BF)
 
     others = PLANE - 1
     all_of(qd.at[0, 0, 0:others], q_send_sem.at[0])
@@ -592,19 +594,35 @@
             rs_copy(0, dst, which, right).wait_send()
 
 
+def owner_sums(dq_parts, kv_parts, dq_out, dk_out, dv_out):
+    for t in range(2):
+        for r in range(0, HQ * D, 512):
+            cols = slice(r, r + 512)
+            total = dq_parts[0, t, :, cols].astype(F32) + dq_parts[1, t, :, cols].astype(F32)
+            dq_out[t * SUB : (t + 1) * SUB, cols] = total.astype(BF)
+    sums = []
+    for which in range(2):
+        total = jnp.zeros((TOK, KVH * D), F32)
+        for kind in range(4):
+            for hh in range(2):
+                total = total + kv_parts[kind, hh, which].astype(F32)
+        sums.append(total)
+    dk_out[...] = (sums[0] * SCALE).astype(BF)
+    dv_out[...] = sums[1].astype(BF)
+
+
 def shards(queries, key_heads, value_heads, outputs, out_grad, log_total, positions):
     vmem = pl.BlockSpec(memory_space=pltpu.VMEM)
     anywhere = pl.BlockSpec(memory_space=pl.ANY)
     dma = pltpu.SemaphoreType.DMA
-    return pl.pallas_call(
+    parts = pl.pallas_call(
         kernel,
         out_shape=(
-            jax.ShapeDtypeStruct((TOK, HQ * D), BF),
-            jax.ShapeDtypeStruct((TOK, KVH * D), BF),
-            jax.ShapeDtypeStruct((TOK, KVH * D), BF),
+            jax.ShapeDtypeStruct((2, 2, SUB, HQ * D), BF),
+            jax.ShapeDtypeStruct((4, 2, 2, TOK, KVH * D), BF),
         ),
         in_specs=[anywhere] * 7,
-        out_specs=(vmem, vmem, vmem),
+        out_specs=(anywhere, anywhere),
         scratch_shapes=[
             pltpu.VMEM((TOK, HQ * D), BF),
             pltpu.VMEM((TOK, KVH * D), BF),
@@ -628,8 +646,6 @@
             pltpu.VMEM((2, 2, HALF, D), BF),
             pltpu.VMEM((Z, 2, PART, D), BF),
             pltpu.VMEM((Z, 2, PART, D), BF),
-            pltpu.VMEM((2, 2, SUB, HQ * D), BF),
-            pltpu.VMEM((4, 2, 2, TOK, KVH * D), BF),
             dma((7,)),
             dma((3,)),
             dma((3,)),
@@ -652,6 +668,16 @@
             collective_id=0, has_side_effects=True, vmem_limit_bytes=60 << 20
         ),
     )(queries, key_heads, value_heads, outputs, out_grad, log_total, positions)
+    return pl.pallas_call(
+        owner_sums,
+        out_shape=(
+            jax.ShapeDtypeStruct((TOK, HQ * D), BF),
+            jax.ShapeDtypeStruct((TOK, KVH * D), BF),
+            jax.ShapeDtypeStruct((TOK, KVH * D), BF),
+        ),
+        in_specs=[vmem, vmem],
+        out_specs=(vmem, vmem, vmem),
+    )(*parts)
 
 
 def solution(mesh):

time: 66.9 us -> 64 us (0.957)
  local copies, waits for them, and re-layouts: 3.06 us -> 0 us
    unnamed x7 -> x0, local copies, waits for them, and re-layouts: 3.06 us -> none
    pallas_call x1 -> x2, Pallas kernels: 63 us -> 63.2 us  [the longest x1 61.2 us: shards(): pl.pallas_call(kernel, out_shape=(jax.ShapeDtypeStruct((2, 2, SUB, HQ * D...]
where the time goes in v5:
time: 64 us; the launch traced here: 63.9 us
  Pallas kernels  63.2 us (99%)
  between operations  0.64 us (1%)
    pallas_call x1, Pallas kernels, shards(): pl.pallas_call(kernel, out_shape=(jax.ShapeDtypeStruct((2, 2, SUB, HQ * D...  61.2 us
    pallas_call x1, Pallas kernels, shards(): pl.pallas_call(owner_sums, out_shape=(jax.ShapeDtypeStruct((TOK, HQ * D),...  2 us

profile of v5, /device:TPU:1, one launch (start us, length us, event | category | flops | bytes accessed | tf_op | source)
XLA Modules:
  0.0 63.9 jit_solution(12030285865322803365)
XLA Ops:
  0.6 61.2 %shard_map.94 = (bf16[2,2,16,4096]{3,2,1,0:T(8,128)(2,1)}, bf16[4,2,2,32,512]{4,3,2,1,0:T(8,128)(2,1)}) custom-call(bf16[32,4096]{1,0:T(8,128)(2,1)} %q_hbm.1, bf16[32,512]{1,0:T(8,128)(2,1)} %k_hbm.1, bf16[32,512]{1,0:T(8,128)(2,1)} %v_hbm.1, bf16[32,4096]{1,0:T(8,128)(2,1)} %o_hbm.1, bf16[32,4096]{1,0:T(8,128)(2,1)} %g_hbm.1, bf16[32,32]{1,0:T(8,128)(2,1)} %lse_hbm.1, ...), custom_call_target="tpu_custom_call" | custom-call | tf_op jit(solution)/shard_map/pallas_call | solution.py:618
  61.9 2.0 %shard_map.95 = (bf16[32,4096]{1,0:T(8,128)(2,1)}, bf16[32,512]{1,0:T(8,128)(2,1)}, bf16[32,512]{1,0:T(8,128)(2,1)}) custom-call(bf16[2,2,16,4096]{3,2,1,0:T(8,128)(2,1)} %get-tuple-element.5.dq_parts, bf16[4,2,2,32,512]{4,3,2,1,0:T(8,128)(2,1)} %get-tuple-element.6.kv_parts), custom_call_target="tpu_custom_call" | custom-call | tf_op jit(solution)/shard_map/pallas_call | solution.py:671

commit v6 on v5

--- a/solution.py
+++ b/solution.py
@@ -364,10 +364,7 @@
 
     def swap_start(k):
         for t in range(2):
-            for r in range(0, HALF, QT):
-                dqx_send[k, t, r : r + QT, :] = (
-                    (dqt[2 * k + 1, t, :, r : r + QT] * SCALE).T.astype(BF)
-                )
+            dqx_send[k, t] = (dqt[2 * k + 1, t] * SCALE).astype(BF)
         swap(k).start()
 
     def dq_columns(k):
@@ -389,10 +386,10 @@
         swap(k).wait_recv()
         for t in range(2):
             for r in range(0, HALF, QT):
-                total = (dqt[2 * k, t, :, r : r + QT] * SCALE).T
-                total = total + dqx[k, t, r : r + QT, :].astype(F32)
+                cols = slice(r, r + QT)
+                total = dqt[2 * k, t, :, cols] * SCALE + dqx[k, t, :, cols].astype(F32)
                 first = r // SUB
-                dqs[k, t, first : first + QT // SUB] = total.astype(BF).reshape(
+                dqs[k, t, first : first + QT // SUB] = total.astype(BF).T.reshape(
                     QT // SUB, SUB, D
                 )
 
@@ -507,7 +504,7 @@
 
     lax.fori_loop(0, 3, halves, 0)
 
-    steps = ((2, 0), (2, 1), (1, 1), (3, 0), (3, 1))
+    steps = ((2, 0), (2, 1), (3, 0), (3, 1), (1, 1))
 
     def step_of(s, carry):
         pair, head = carry[0] % 4, 2 * (carry[1] % 2)
@@ -530,16 +527,17 @@
         def _():
             reduce_step(5, True)
             reduce_step(3, True)
+            ring_step(3)
 
         @pl.when(s == 3)
         def _():
-            ring_step(3)
+            swap_start(0)
 
         @pl.when(s == 4)
         def _():
-            reduce_step(6, False)
-            reduce_step(2, False)
-            swap_start(0)
+            out_direct(4)
+            out_direct(0)
+            send_dq(0)
 
         attend((head, head + 1), (0, 1), (7 - pair, (1 + pair) % 4))
         return carry[0] // 4, carry[1] // 2
@@ -553,9 +551,8 @@
             jnp.int32(sum(head * 2**s for s, (_, head) in enumerate(steps))),
         ),
     )
-    out_direct(4)
-    out_direct(0)
-    send_dq(0)
+    reduce_step(6, False)
+    reduce_step(2, False)
 
     def last(u, carry):
         attend((3 - u,), (0, 1), (7, 1))
@@ -567,9 +564,9 @@
         return carry
 
     lax.fori_loop(0, 2, last, 0)
+    send_dq(1)
     reduce_step(1, False)
     reduce_step(7, False)
-    send_dq(1)
 
     all_of(dq_recv, dq_recv_sem)
     all_of(kv_recv, out_recv_sem)
@@ -642,8 +639,8 @@
             pltpu.VMEM((Z, 2, PART, D), F32),
             pltpu.VMEM((LOCAL, 2, D, HALF), F32),
             pltpu.VMEM((2, 2, PLANE, SUB, D), BF),
-            pltpu.VMEM((2, 2, HALF, D), BF),
-            pltpu.VMEM((2, 2, HALF, D), BF),
+            pltpu.VMEM((2, 2, D, HALF), BF),
+            pltpu.VMEM((2, 2, D, HALF), BF),
             pltpu.VMEM((Z, 2, PART, D), BF),
             pltpu.VMEM((Z, 2, PART, D), BF),
             dma((7,)),

time: 64 us -> 63.2 us (0.988)
  Pallas kernels: 63.2 us -> 62.4 us
    pallas_call x1, Pallas kernels: 61.2 us -> 60.4 us  [shards(): pl.pallas_call(kernel, out_shape=(jax.ShapeDtypeStruct((2, 2, SUB, HQ * D...]
where the time goes in v6:
time: 63.2 us; the launch traced here: 63.1 us
  Pallas kernels  62.4 us (99%)
  between operations  0.64 us (1%)
    pallas_call x1, Pallas kernels, shards(): pl.pallas_call(kernel, out_shape=(jax.ShapeDtypeStruct((2, 2, SUB, HQ * D...  60.4 us
    pallas_call x1, Pallas kernels, shards(): pl.pallas_call(owner_sums, out_shape=(jax.ShapeDtypeStruct((TOK, HQ * D),...  2 us

profile of v6, /device:TPU:1, one launch (start us, length us, event | category | flops | bytes accessed | tf_op | source)
XLA Modules:
  0.0 63.1 jit_solution(14573794240768845857)
XLA Ops:
  0.6 60.4 %shard_map.94 = (bf16[2,2,16,4096]{3,2,1,0:T(8,128)(2,1)}, bf16[4,2,2,32,512]{4,3,2,1,0:T(8,128)(2,1)}) custom-call(bf16[32,4096]{1,0:T(8,128)(2,1)} %q_hbm.1, bf16[32,512]{1,0:T(8,128)(2,1)} %k_hbm.1, bf16[32,512]{1,0:T(8,128)(2,1)} %v_hbm.1, bf16[32,4096]{1,0:T(8,128)(2,1)} %o_hbm.1, bf16[32,4096]{1,0:T(8,128)(2,1)} %g_hbm.1, bf16[32,32]{1,0:T(8,128)(2,1)} %lse_hbm.1, ...), custom_call_target="tpu_custom_call" | custom-call | tf_op jit(solution)/shard_map/pallas_call | solution.py:615
  61.1 2.0 %shard_map.95 = (bf16[32,4096]{1,0:T(8,128)(2,1)}, bf16[32,512]{1,0:T(8,128)(2,1)}, bf16[32,512]{1,0:T(8,128)(2,1)}) custom-call(bf16[2,2,16,4096]{3,2,1,0:T(8,128)(2,1)} %get-tuple-element.5.dq_parts, bf16[4,2,2,32,512]{4,3,2,1,0:T(8,128)(2,1)} %get-tuple-element.6.kv_parts), custom_call_target="tpu_custom_call" | custom-call | tf_op jit(solution)/shard_map/pallas_call | solution.py:668

commit v7 on v6

--- a/solution.py
+++ b/solution.py
@@ -236,7 +236,7 @@
         return pltpu.make_async_remote_copy(
             src_ref=kv.at[src, which],
             dst_ref=kv.at[dst, which],
-            send_sem=ring_send_sem.at[which, dst],
+            send_sem=ring_send_sem.at[which],
             recv_sem=ring_recv_sem.at[which, dst],
             device_id=device,
             device_id_type=MESH,
@@ -419,7 +419,7 @@
         return pltpu.make_async_remote_copy(
             src_ref=rs_send.at[src, which],
             dst_ref=rs.at[dst, which],
-            send_sem=rs_send_sem.at[which, dst],
+            send_sem=rs_send_sem.at[which],
             recv_sem=rs_recv_sem.at[which, dst],
             device_id=device,
             device_id_type=MESH,
@@ -585,10 +585,8 @@
     for stage in range(3):
         forward(stage).wait_send()
     for which in range(2):
-        for dst in range(1, 8):
-            ring_copy(0, dst, which, right).wait_send()
-        for dst in (1, 2, 6, 7):
-            rs_copy(0, dst, which, right).wait_send()
+        all_of(kv.at[1:8, which], ring_send_sem.at[which])
+        all_of(rs.at[0:4, which], rs_send_sem.at[which])
 
 
 def owner_sums(dq_parts, kv_parts, dq_out, dk_out, dv_out):
@@ -650,9 +648,9 @@
             dma((3,)),
             dma,
             dma,
+            dma((2,)),
             dma((2, Z)),
-            dma((2, Z)),
-            dma((2, Z)),
+            dma((2,)),
             dma((2, Z)),
             dma((2,)),
             dma((2,)),

time: 63.2 us -> 62.9 us (level)
  no operation moved by 1% of the time
where the time goes in v7:
time: 62.9 us; the launch traced here: 62.8 us
  Pallas kernels  62.1 us (99%)
  between operations  0.64 us (1%)
    pallas_call x1, Pallas kernels, shards(): pl.pallas_call(kernel, out_shape=(jax.ShapeDtypeStruct((2, 2, SUB, HQ * D...  60.1 us
    pallas_call x1, Pallas kernels, shards(): pl.pallas_call(owner_sums, out_shape=(jax.ShapeDtypeStruct((TOK, HQ * D),...  2 us

profile of v7, /device:TPU:1, one launch (start us, length us, event | category | flops | bytes accessed | tf_op | source)
XLA Modules:
  0.0 62.8 jit_solution(1151562223906332585)
XLA Ops:
  0.6 60.1 %shard_map.94 = (bf16[2,2,16,4096]{3,2,1,0:T(8,128)(2,1)}, bf16[4,2,2,32,512]{4,3,2,1,0:T(8,128)(2,1)}) custom-call(bf16[32,4096]{1,0:T(8,128)(2,1)} %q_hbm.1, bf16[32,512]{1,0:T(8,128)(2,1)} %k_hbm.1, bf16[32,512]{1,0:T(8,128)(2,1)} %v_hbm.1, bf16[32,4096]{1,0:T(8,128)(2,1)} %o_hbm.1, bf16[32,4096]{1,0:T(8,128)(2,1)} %g_hbm.1, bf16[32,32]{1,0:T(8,128)(2,1)} %lse_hbm.1, ...), custom_call_target="tpu_custom_call" | custom-call | tf_op jit(solution)/shard_map/pallas_call | solution.py:613
  60.8 2.0 %shard_map.95 = (bf16[32,4096]{1,0:T(8,128)(2,1)}, bf16[32,512]{1,0:T(8,128)(2,1)}, bf16[32,512]{1,0:T(8,128)(2,1)}) custom-call(bf16[2,2,16,4096]{3,2,1,0:T(8,128)(2,1)} %get-tuple-element.5.dq_parts, bf16[4,2,2,32,512]{4,3,2,1,0:T(8,128)(2,1)} %get-tuple-element.6.kv_parts), custom_call_target="tpu_custom_call" | custom-call | tf_op jit(solution)/shard_map/pallas_call | solution.py:666
